TPU v7x, 768 devices: a whole 4x8x12 slice. The times are simulated.
768 devices in a mesh: group: 64 (over x, y, core), dp: 12 (over z).
Axes of the slice: x: 4, y: 8, z: 12, core: 2. Of those that a mesh axis runs over, the one named last changes fastest.
Arguments:
- hidden: bfloat16 [64, 3072, 4096], P('group', 'dp'), may hold values from -6 to 6
- segment_ids: int32 [64, 12, 256], P('group', 'dp'), may hold values from 0 to 3, never falling along the last dimension, each value on 1 to 160 neighbouring positions
- assign: int32 [64, 48], P('group', 'dp'), may hold values from 0 to 47, each once within a row
- positive: int32 [64, 48], P(None, 'dp'), may hold values from 0 to 255, as said below
- gain: float32 [4096], replicated, may hold values from 0.1 to 1.9
Outputs:
- query_loss: float32 [64, 48], P('group', 'dp')
- grad_rows: bfloat16 [64, 3072, 4096], P('group', 'dp')
Inputs may be any that keep to these rules, and one draw needn't show every extreme that they name: `segment_ids`: each passage is a run of rows of one device, every local passage has one row or more, and one passage per device has exactly 160 rows. Each row of assign is a permutation; value v names owner device v // 4 along dp and its slot v % 4. A passage's positive is never itself.
All inputs are finite; a program needn't handle non-finite values.
Results may differ from a plain program's by a relative error of at most 0.0067.
Values may be sent and summed in bfloat16 or wider, within the bound.
No kernel may reach another device: no remote copies, remote signals or barrier semaphores. Data moves between devices by JAX's collectives and lax.ppermute only.
A program may use at most 64 MiB of HBM per device.

v0:
```python
import jax
import jax.numpy as jnp
from jax import lax
from jax.sharding import PartitionSpec as P

inv_tau = 20.0
loss_scale = 1024.0
norm_eps = 1e-06


def local(hidden, segment_ids, assign, positive, gain):
    rows_in = hidden[0]
    segment_row = segment_ids[0, 0]
    assign_row = assign[0]
    passages = assign_row.shape[0]
    width = rows_in.shape[1]
    values = rows_in.astype(jnp.float32)
    inverse = lax.rsqrt(jnp.mean(values * values, axis=-1, keepdims=True) + norm_eps)
    normed = values * inverse * gain
    onehot = (segment_row[None, :] == jnp.arange(passages)[:, None]).astype(jnp.float32)
    counts = jnp.sum(onehot, axis=1)
    pooled = jnp.dot(
        onehot, normed, precision=lax.Precision.HIGHEST, preferred_element_type=jnp.float32
    )
    pooled = (pooled / counts[:, None]).astype(jnp.bfloat16)
    peers = lax.axis_size("dp")
    owned_count = peers * passages
    placing = (assign_row[None, :] == jnp.arange(owned_count)[:, None]).astype(jnp.bfloat16)
    pooled_all, assign_all = (
        lax.all_gather(pooled, "dp", axis=0, tiled=True),
        lax.all_gather(assign_row, "dp", axis=0, tiled=True),
    )
    wanted = lax.axis_index("dp") * passages + jnp.arange(passages)
    select = (assign_all[None, :] == wanted[:, None]).astype(jnp.bfloat16)
    own_embed = jnp.dot(select, pooled_all, preferred_element_type=jnp.float32).astype(jnp.bfloat16)
    every_embed = lax.all_gather(own_embed, "group", axis=0, tiled=True)
    batch_size = every_embed.shape[0]
    every_values = every_embed.astype(jnp.float32)
    lengths = jnp.sqrt(jnp.sum(every_values * every_values, axis=-1, keepdims=True) + norm_eps)
    unit = every_values / lengths
    unit_bf = unit.astype(jnp.bfloat16)
    member = lax.axis_index("group")
    first = member * passages
    own_unit = lax.dynamic_slice_in_dim(unit, first, passages, 0)
    own_unit_bf = lax.dynamic_slice_in_dim(unit_bf, first, passages, 0)
    own_length = lax.dynamic_slice_in_dim(lengths, first, passages, 0)
    query_index = first + jnp.arange(passages)
    columns = jnp.arange(batch_size)
    logits = jnp.dot(own_unit_bf, unit_bf.T, preferred_element_type=jnp.float32) * inv_tau
    logits = jnp.where(columns[None, :] == query_index[:, None], -1e30, logits)
    top = jnp.max(logits, axis=-1, keepdims=True)
    lse = top[:, 0] + jnp.log(jnp.sum(jnp.exp(logits - top), axis=-1))
    partners = positive.reshape(-1)
    own_partner = lax.dynamic_slice_in_dim(partners, first, passages, 0)
    hits = columns[None, :] == own_partner[:, None]
    target = jnp.sum(jnp.where(hits, logits, 0.0), axis=-1)
    query_loss = lse - target
    prob = jnp.exp(logits - lse[:, None])
    weights = (loss_scale * (prob - hits.astype(jnp.float32))).astype(jnp.bfloat16)
    grad_own = jnp.dot(weights, unit_bf, preferred_element_type=jnp.float32) * inv_tau
    grad_key = lax.psum_scatter(
        jnp.dot(weights.T, own_unit_bf, preferred_element_type=jnp.float32) * inv_tau,
        "group",
        scatter_dimension=0,
        tiled=True,
    )
    grad_unit = grad_own + grad_key
    inner = jnp.sum(own_unit * grad_unit, axis=-1, keepdims=True)
    grad_embed = ((grad_unit - own_unit * inner) / own_length).astype(jnp.bfloat16)
    grad_all = lax.all_gather(grad_embed, "dp", axis=0, tiled=True)
    grad_local = jnp.dot(placing.T, grad_all, preferred_element_type=jnp.float32)
    scaled = grad_local / counts[:, None]
    spread = jnp.dot(
        onehot.T, scaled, precision=lax.Precision.HIGHEST, preferred_element_type=jnp.float32
    )
    gained = gain * spread
    grad = inverse * gained - values * inverse**3 * jnp.mean(
        values * gained, axis=-1, keepdims=True
    )
    return (
        query_loss.reshape(1, passages),
        grad.astype(jnp.bfloat16).reshape(1, rows_in.shape[0], width),
    )


def solution(mesh):
    placed = (P("group", "dp", None), P("group", "dp", None), P("group", "dp"), P(None, "dp"), P())
    return jax.shard_map(
        local,
        mesh=mesh,
        in_specs=placed,
        out_specs=(P("group", "dp"), P("group", "dp", None)),
        check_vma=False,
    )
```

profile of v0, /device:TPU:1, one launch (start us, length us, event | category | flops | bytes accessed | tf_op | source)
XLA Modules:
  0.0 423.7 jit_solution(4282007356718820986)
XLA Ops:
  7.2 0.0 copy-start.5
  7.2 0.0 copy-start.3
  7.2 0.0 all-gather.6.cloned.1.call-start
  7.2 2.1 fusion.4
  9.3 0.8 convert_reduce_fusion
  10.1 3.5 fusion.3
  13.6 30.3 %all-gather.1 = bf16[12,4,4096]{2,1,0:T(4,128)(2,1)S(1)} all-gather(bf16[1,4,4096]{2,1,0:T(4,128)(2,1)S(1)} %fusion.3), channel_id=1, replica_groups=mesh['group'=64,'dp'=12] {'dp'}, dimensions={0}, use_global_device_ids=true | all-gather | bytes 425984 | tf_op jit(solution)/shard_map/all_gather | solution.py:30
  43.9 0.1 reshape.101
  44.0 1.3 dynamic-slice.4
  45.9 0.0 copy-done.5
  45.9 0.1 bitcast_dynamic-update-slice_fusion
  46.0 15.4 %all-reduce = s32[48]{0:T(128)S(1)} all-reduce(s32[48]{0:T(128)S(1)} %bitcast_dynamic-update-slice_fusion), channel_id=2, replica_groups=mesh['group'=64,'dp'=12] {'dp'}, use_global_device_ids=true, to_apply=%add | all-reduce | flops 48 | bytes 384
  61.4 0.8 fusion.2
  62.3 0.0 all-gather.6.cloned.1.call-update
  62.3 0.0 all-reduce.4.cloned.1.call-start
  62.4 0.0 copy-done.3
  62.4 0.1 copy.9
  62.5 0.1 reshape.93
  62.6 0.1 dynamic_slice.11
  62.6 94.4 %all-gather.6.cloned.1.call-done = bf16[64,4,4096]{2,1,0:T(4,128)(2,1)} async-done(((bf16[1,4,4096]{2,1,0:T(4,128)(2,1)}), bf16[64,4,4096]{2,1,0:T(4,128)(2,1)}) %all-gather.6.cloned.1.call-update) | async-done | bytes 2097168 | tf_op jit(solution)/shard_map/all_gather | solution.py:36
  157.0 4.2 reshape.106
  161.2 0.0 copy-start
  161.2 2.7 multiply_reduce_fusion
  163.9 0.7 copy-done
  164.7 2.8 fusion.28
  167.4 0.8 fusion.29
  168.2 0.2 select_reduce_fusion
  168.4 0.5 subtract_bitcast_fusion
  169.0 2.8 convolution_multiply_fusion.1
  171.8 0.0 copy-start.2
  171.8 0.0 copy-start.4
  171.8 0.0 all-reduce.4.cloned.1.call-update
  171.8 1.3 dynamic-slice.5
  173.7 0.1 dynamic-slice.3
  173.8 211.8 %all-reduce.4.cloned.1.call-done = f32[256,4096]{1,0:T(8,128)} async-done(((f32[256,4096]{1,0:T(8,128)}), f32[256,4096]{1,0:T(8,128)}) %all-reduce.4.cloned.1.call-update) | async-done | bytes 4194320
  385.7 1.5 multiply_reduce_fusion.1
  387.2 0.0 copy-start.1
  387.2 1.2 fusion.17
  388.3 21.5 %all-gather.3 = bf16[12,4,4096]{2,1,0:T(4,128)(2,1)S(1)} all-gather(bf16[1,4,4096]{2,1,0:T(4,128)(2,1)S(1)} %fusion.17), channel_id=1, replica_groups=mesh['group'=64,'dp'=12] {'dp'}, dimensions={0}, use_global_device_ids=true | all-gather | bytes 425984 | tf_op jit(solution)/shard_map/all_gather | solution.py:70
  409.9 0.1 reshape.105
  409.9 0.2 convolution_divide_fusion
  410.2 0.0 copy-done.2
  410.2 0.0 copy-done.4
  410.2 3.9 fusion.10
  414.1 0.0 copy-done.1
  414.1 2.7 fusion.11
  (6 shorter events, 0.0 us)
Async XLA Ops:
  7.2 38.8 %copy-start.5 = (s32[1,4]{1,0:T(1,128)S(1)}, s32[1,4]{1,0:T(1,128)}, u32[]{:S(2)}) copy-start(s32[1,4]{1,0:T(1,128)} %param.7) | copy-start | bytes 52
  7.2 55.2 %copy-start.3 = (s32[64,4]{0,1:T(4,128)S(1)}, s32[64,4]{0,1:T(4,128)}, u32[]{:S(2)}) copy-start(s32[64,4]{0,1:T(4,128)} %param.8) | copy-start | bytes 3076
  7.2 149.8 %all-gather.6.cloned.1.call-start = ((), (), s32[]{:S(2)}) async-start(), calls=%async_computation | async-start | bytes 2129920 | tf_op jit(solution)/shard_map/all_gather | solution.py:36
  62.3 323.4 %all-reduce.4.cloned.1.call-start = ((), (), s32[]{:S(2)}) async-start(), calls=%async_computation.1 | async-start | bytes 8388608
  161.2 3.4 copy-start
  171.8 238.4 %copy-start.2 = (f32[4096]{0:T(1024)S(1)}, f32[4096]{0:T(1024)}, u32[]{:S(2)}) copy-start(f32[4096]{0:T(1024)} %param.9) | copy-start | bytes 49156
  171.8 238.4 %copy-start.4 = (s32[1,1,256]{2,1,0:T(1,128)S(1)}, s32[1,1,256]{2,1,0:T(1,128)}, u32[]{:S(2)}) copy-start(s32[1,1,256]{2,1,0:T(1,128)} %param.6) | copy-start | bytes 3076
  387.2 26.9 %copy-start.1 = (bf16[1,256,4096]{2,1,0:T(8,128)(2,1)S(1)}, bf16[1,256,4096]{2,1,0:T(8,128)(2,1)}, u32[]{:S(2)}) copy-start(bf16[1,256,4096]{2,1,0:T(8,128)(2,1)} %param.5) | copy-start | bytes 6291460
Sparse Core Ops, SparseCore 0:
  62.4 94.5 all-gather.5
  171.9 213.6 all-reduce.3
where the time goes:
time: 429 us; the launch traced here: 424 us
  waiting for transfers between devices  306 us (71%)
  blocking collectives  67.2 us (16%)
  between operations  15.5 us (4%)
  matrix products  13.5 us (3%)
  other arithmetic  13 us (3%)
  local copies, waits for them, and re-layouts  8.18 us (2%)
    unnamed x3, waiting for transfers between devices  212 us
    all_gather x1, waiting for transfers between devices, local(): every_embed = lax.all_gather(own_embed, 'group', axis=0, tiled=True)  94.4 us
    all_gather x1, blocking collectives, local(): lax.all_gather(pooled, 'dp', axis=0, tiled=True)  30.3 us
    all_gather x1, blocking collectives, local(): grad_all = lax.all_gather(grad_embed, 'dp', axis=0, tiled=True)  21.5 us
    unnamed x1, blocking collectives  15.4 us
  transfers between devices with their start and end apart: 2, of which 2 were waited for; matrix products, arithmetic and copies ran while one was open for 0% of the time, Pallas kernels for 0%

commit v1 on v0

v1 whole, which is shorter than its diff:
```python
import functools

import jax
import jax.numpy as jnp
from jax import lax
from jax.experimental import pallas as pl
from jax.experimental.pallas import tpu as pltpu
from jax.sharding import Mesh
from jax.sharding import PartitionSpec as P

inv_tau = 20.0
loss_scale = 1024.0
norm_eps = 1e-06

F32 = jnp.float32
BF16 = jnp.bfloat16
ROWS = 256
D = 4096
HALF = D // 2
PAS = 4
META = 128
N_DP = 12
N_XY = 32
BATCH = 256

VMEM = pl.BlockSpec(memory_space=pltpu.VMEM)
SMEM = pl.BlockSpec(memory_space=pltpu.SMEM)
PARAMS = pltpu.CompilerParams(vmem_limit_bytes=40 * 1024 * 1024)


def iota(shape, dim):
    return lax.broadcasted_iota(jnp.int32, shape, dim)


def split3(values):
    high = values.astype(BF16).astype(F32)
    rest = values - high
    middle = rest.astype(BF16).astype(F32)
    low = rest - middle
    return jnp.concatenate([high, middle, low], axis=0).astype(BF16)


def sum3(values):
    return values[0:8] + values[8:16] + values[16:24]


def pool_kernel(hidden_ref, segment_ref, assign_ref, gain_ref, send_ref, inverse_ref, squares):
    def block(at, carry):
        rows = pl.ds(pl.multiple_of(at * 16, 16), 16)
        values = hidden_ref[0, rows, :].astype(F32)
        total = jnp.sum(values * values, axis=1, keepdims=True)
        squares[rows, :] = jnp.broadcast_to(total, (16, 128))
        return carry

    lax.fori_loop(0, ROWS // 16, block, 0)
    inverse = lax.rsqrt(squares[...].T[0:8] * (1.0 / D) + norm_eps)
    inverse_ref[...] = inverse
    segment = jnp.broadcast_to(segment_ref[0], (8, ROWS))
    onehot = jnp.where(segment == iota((8, ROWS), 0), 1.0, 0.0)
    counts = jnp.maximum(jnp.sum(onehot, axis=1, keepdims=True), 1.0)
    weights = split3(onehot * inverse)
    slot = iota((8, META), 0)
    meta = jnp.zeros((8, META), F32)
    for k in range(PAS):
        meta = jnp.where(lax.rem(slot, PAS) == k, assign_ref[0, k].astype(F32), meta)
    lane = lax.axis_index("dp") * 8 + slot
    meta = jnp.where(iota((8, META), 1) == lane, meta, 0.0).astype(BF16)
    halves = []
    for h in range(2):
        columns = pl.ds(h * HALF, HALF)
        pooled = sum3(jnp.dot(weights, hidden_ref[0, :, columns], preferred_element_type=F32))
        halves.append((pooled * gain_ref[:, columns] / counts)[0:PAS])
    packed = jnp.concatenate(halves, axis=0).astype(BF16)
    for peer in range(N_DP):
        send_ref[peer, :, 0:HALF] = packed
        send_ref[peer, :, HALF:] = meta


def unit_kernel(pooled_ref, send_ref, embed_ref, length_ref):
    core = lax.axis_index("core")
    wanted = lax.axis_index("dp") * PAS
    row = iota((8, META), 0)
    lane = iota((8, META), 1)
    embeds, lengths = [], []
    for c in range(2):
        owners = jnp.sum(pooled_ref[c, :, HALF:].astype(F32), axis=0, keepdims=True)
        hit = (owners == (wanted + lax.rem(row, PAS)).astype(F32)) & (
            lax.div(lax.rem(lane, 8), PAS) == lax.div(row, PAS)
        )
        select = jnp.where(hit & (lane < N_DP * 8), 1.0, 0.0)[:, : N_DP * 8].astype(BF16)
        embed = jnp.dot(select, pooled_ref[c, :, 0:HALF], preferred_element_type=F32)
        squares = jnp.sum(embed * embed, axis=1, keepdims=True)
        squares = squares[0:PAS] + squares[PAS:]
        embeds.append(embed)
        lengths.append(jnp.sqrt(squares + norm_eps))
    length = jnp.concatenate(lengths, axis=0)
    own = jnp.where(
        core == 0,
        jnp.concatenate([embeds[0][0:PAS], embeds[1][0:PAS]], axis=0),
        jnp.concatenate([embeds[0][PAS:], embeds[1][PAS:]], axis=0),
    )
    embed_ref[...] = own
    length_ref[...] = jnp.broadcast_to(length, (8, 128))
    unit = (own / length).astype(BF16)
    for peer in range(N_XY):
        send_ref[peer] = unit


def gram_kernel(unit_ref, embed_ref, gram_ref):
    units = unit_ref[...]
    dims = (((1,), (1,)), ((), ()))
    gram_ref[0:BATCH] = lax.dot_general(units, units, dims, preferred_element_type=F32)
    gram_ref[BATCH:] = lax.dot_general(
        embed_ref[...].astype(BF16), units, dims, preferred_element_type=F32
    )


def contrast_kernel(gram_ref, unit_ref, embed_ref, length_ref, positive_ref, loss_ref, send_ref):
    core = lax.axis_index("core")
    first = (lax.axis_index("x") * 8 + lax.axis_index("y")) * 8
    shift = inv_tau
    row = iota((8, BATCH), 0)
    lane = iota((8, BATCH), 1)
    mine = first + row
    lanes = iota((64, BATCH), 1)
    partner = jnp.zeros((64, BATCH), jnp.int32)
    for s in range(PAS):
        partner = jnp.where(lax.rem(lanes, PAS) == s, positive_ref[:, s : s + 1], partner)
    partner = jnp.where(lax.div(lanes, PAS) == iota((64, BATCH), 0), partner, 0)
    partner = jnp.sum(partner, axis=0, keepdims=True)
    own_partner = jnp.sum(jnp.where(lane == mine, partner, 0), axis=1, keepdims=True)

    logits = (gram_ref[0, 0:BATCH] + gram_ref[1, 0:BATCH]) * inv_tau
    everyone = iota((BATCH, BATCH), 0) == iota((BATCH, BATCH), 1)
    logits = jnp.where(everyone, -1e30, logits)
    lse_all = shift + jnp.log(jnp.sum(jnp.exp(logits - shift), axis=0, keepdims=True))
    at = pl.ds(pl.multiple_of(first, 8), 8)
    own = (gram_ref[0, at, :] + gram_ref[1, at, :]) * inv_tau
    own = jnp.where(lane == mine, -1e30, own)
    lse = shift + jnp.log(jnp.sum(jnp.exp(own - shift), axis=1, keepdims=True))
    hits = lane == own_partner
    loss = lse - jnp.sum(jnp.where(hits, own, 0.0), axis=1, keepdims=True)
    as_query = loss_scale * (jnp.exp(own - lse) - jnp.where(hits, 1.0, 0.0))
    as_key = loss_scale * (jnp.exp(own - lse_all) - jnp.where(partner == mine, 1.0, 0.0))
    weights = jnp.concatenate([as_query, as_key], axis=0).astype(BF16)
    grad = jnp.dot(weights, unit_ref[...], preferred_element_type=F32)
    grad = (grad[0:8] + grad[8:16]) * inv_tau
    weights = weights.astype(F32)
    length = length_ref[:, 0:1]
    along = (gram_ref[0, BATCH:] + gram_ref[1, BATCH:]) / length
    inner = inv_tau * jnp.sum((weights[0:8] + weights[8:16]) * along, axis=1, keepdims=True)
    grad = ((grad - embed_ref[...] / length * inner) / length).astype(BF16)
    for peer in range(N_DP):
        send_ref[peer] = grad
    place = (iota((8, 128), 1) + core * PAS) == iota((8, 128), 0)
    loss = jnp.sum(jnp.where(place, loss, 0.0), axis=0, keepdims=True)
    loss_ref[...] = loss[:, 0:PAS]


def rows_kernel(
    grad_ref, hidden_ref, segment_ref, assign_ref, gain_ref, inverse_ref, out_ref, scaled, coef
):
    core = lax.axis_index("core")
    row = iota((8, N_DP * 8), 0)
    lane = iota((8, N_DP * 8), 1)
    select = jnp.zeros((8, N_DP * 8), F32)
    for k in range(PAS):
        owner = assign_ref[0, k]
        at = lax.div(owner, PAS) * 8 + core * PAS + lax.rem(owner, PAS)
        select = jnp.where((row == k) & (lane == at), 1.0, select)
    select = select.astype(BF16)
    segment = jnp.broadcast_to(segment_ref[0], (8, ROWS))
    onehot = jnp.where(segment == iota((8, ROWS), 0), 1.0, 0.0)
    counts = jnp.maximum(jnp.sum(onehot, axis=1, keepdims=True), 1.0)
    for h in range(2):
        columns = pl.ds(h * HALF, HALF)
        part = jnp.dot(select, grad_ref[h], preferred_element_type=F32)
        scaled[:, columns] = split3(gain_ref[:, columns] * (part / counts))
    upright = jnp.concatenate(
        [onehot, onehot, onehot, inverse_ref[...], jnp.zeros((96, ROWS), F32)], axis=0
    ).T
    spread = upright[:, 0:24]
    inverse = upright[:, 24:25]
    dots = lax.dot_general(
        hidden_ref[0], scaled[...], (((1,), (1,)), ((), ())), preferred_element_type=F32
    )
    dot = jnp.sum(dots * spread, axis=1, keepdims=True) * (1.0 / D)
    coef[:, 0:128] = jnp.broadcast_to(inverse, (ROWS, 128))
    coef[:, 128:256] = jnp.broadcast_to(inverse * inverse * inverse * dot, (ROWS, 128))
    spread = spread.astype(BF16)
    width = 512
    for at in range(0, D, width):
        columns = pl.ds(at, width)
        gained = jnp.dot(spread, scaled[:, columns], preferred_element_type=F32)
        values = hidden_ref[0, :, columns].astype(F32)
        out_ref[0, :, columns] = (
            coef[:, 0:1] * gained - values * coef[:, 128:129]
        ).astype(BF16)


def local(hidden, segment_ids, assign, positive, gain):
    shape = jax.ShapeDtypeStruct
    gain = gain.reshape(1, D)
    with jax.named_scope("pool"):
        send, inverse = pl.pallas_call(
            pool_kernel,
            out_shape=(shape((N_DP, 8, HALF + META), BF16), shape((8, ROWS), F32)),
            in_specs=[VMEM, VMEM, SMEM, VMEM],
            out_specs=(VMEM, VMEM),
            scratch_shapes=[pltpu.VMEM((ROWS, 128), F32)],
            compiler_params=PARAMS,
        )(hidden, segment_ids, assign, gain)
    with jax.named_scope("pooled_exchange"):
        pooled = lax.all_to_all(send, "dp", 0, 0)
        pooled = lax.all_gather(pooled.reshape(N_DP * 8, HALF + META), "core", axis=0)
    with jax.named_scope("unit"):
        send, embed, length = pl.pallas_call(
            unit_kernel,
            out_shape=(shape((N_XY, 8, HALF), BF16), shape((8, HALF), F32), shape((8, 128), F32)),
            in_specs=[VMEM],
            out_specs=(VMEM, VMEM, VMEM),
            compiler_params=PARAMS,
        )(pooled)
    with jax.named_scope("unit_exchange"):
        units = lax.all_to_all(send, ("x", "y"), 0, 0).reshape(BATCH, HALF)
    with jax.named_scope("gram"):
        gram = pl.pallas_call(
            gram_kernel,
            out_shape=shape((BATCH + 8, BATCH), F32),
            in_specs=[VMEM, VMEM],
            out_specs=VMEM,
            compiler_params=PARAMS,
        )(units, embed)
        gram = lax.all_gather(gram, "core", axis=0)
    with jax.named_scope("contrast"):
        loss, send = pl.pallas_call(
            contrast_kernel,
            out_shape=(shape((1, PAS), F32), shape((N_DP, 8, HALF), BF16)),
            in_specs=[VMEM] * 5,
            out_specs=(VMEM, VMEM),
            compiler_params=PARAMS,
        )(gram, units, embed, length, positive)
    with jax.named_scope("grad_exchange"):
        grads = lax.all_to_all(send, "dp", 0, 0)
        grads = lax.all_gather(grads.reshape(N_DP * 8, HALF), "core", axis=0)
    with jax.named_scope("rows"):
        grad_rows = pl.pallas_call(
            rows_kernel,
            out_shape=shape((1, ROWS, D), BF16),
            in_specs=[VMEM, VMEM, VMEM, SMEM, VMEM, VMEM],
            out_specs=VMEM,
            scratch_shapes=[pltpu.VMEM((24, D), BF16), pltpu.VMEM((ROWS, 256), F32)],
            compiler_params=PARAMS,
        )(grads, hidden, segment_ids, assign, gain, inverse)
    return loss, grad_rows


def solution(mesh):
    fine = Mesh(mesh.devices.reshape(4, 8, 2, N_DP), ("x", "y", "core", "dp"))
    group = ("x", "y", "core")
    placed = (P(group, "dp", None), P(group, "dp", None), P(group, "dp"), P(None, "dp"), P())
    return jax.shard_map(
        local,
        mesh=fine,
        in_specs=placed,
        out_specs=(P(group, "dp"), P(group, "dp", None)),
        check_vma=False,
    )
```

time: 429 us -> 121 us (0.28); the launches traced: 424 us -> 121 us
  waiting for transfers between devices: 306 us -> 25.1 us
  between operations: 15.5 us -> 0.71 us
  matrix products: 13.5 us -> 0 us
  other arithmetic: 13 us -> 0 us
  Pallas kernels: 0 us -> 9.87 us
  starting transfers between devices: 0.08 us -> 9.67 us
  blocking collectives: 67.2 us -> 71.8 us
  local copies, waits for them, and re-layouts: 8.18 us -> 3.76 us
    unnamed x3 -> x0, waiting for transfers between devices: 212 us -> none
    all_gather x1 -> x0, waiting for transfers between devices: 94.4 us -> none  [local(): every_embed = lax.all_gather(own_embed, 'group', axis=0, tiled=True)]
    all_to_all x0 -> x2, blocking collectives: none -> 55.7 us  [the longest x1 34.8 us: local(): pooled = lax.all_to_all(send, 'dp', 0, 0)]
    all_gather x2 -> x3, blocking collectives: 51.8 us -> 16.1 us  [the longest x1 6.32 us: local(): gram = lax.all_gather(gram, 'core', axis=0)]
    all_to_all x0 -> x1, waiting for transfers between devices: none -> 25.1 us  [local(): units = lax.all_to_all(send, ('x', 'y'), 0, 0).reshape(BATCH, HALF)]
    unnamed x1 -> x0, blocking collectives: 15.4 us -> none
    dot_general x7 -> x0, matrix products: 13.5 us -> none  [the longest x1 3.91 us: local(): jnp.dot(onehot.T, scaled, precision=lax.Precision.HIGHEST, preferred_elem...]
    pallas_call x0 -> x5, Pallas kernels: none -> 9.87 us  [the longest x1 4.02 us: local(): pl.pallas_call(rows_kernel, out_shape=shape((1, ROWS, D), BF16), in_specs...]
  transfers between devices with their start and end apart: 2 -> 1, of which waited for: 2 -> 1; matrix products, arithmetic and copies ran while one was open for 0% -> 0% of each run, Pallas kernels for 0% -> 0%
where the time goes in v1:
time: 121 us
  blocking collectives  71.8 us (59%)
  waiting for transfers between devices  25.1 us (21%)
  Pallas kernels  9.87 us (8%)
  starting transfers between devices  9.67 us (8%)
  local copies, waits for them, and re-layouts  3.76 us (3%)
    all_to_all x1, blocking collectives, local(): pooled = lax.all_to_all(send, 'dp', 0, 0)  34.8 us
    all_to_all x1, waiting for transfers between devices, local(): units = lax.all_to_all(send, ('x', 'y'), 0, 0).reshape(BATCH, HALF)  25.1 us
    all_to_all x1, blocking collectives, local(): grads = lax.all_to_all(send, 'dp', 0, 0)  20.9 us
    all_to_all x1, starting transfers between devices, local(): units = lax.all_to_all(send, ('x', 'y'), 0, 0).reshape(BATCH, HALF)  9.67 us
    all_gather x1, blocking collectives, local(): gram = lax.all_gather(gram, 'core', axis=0)  6.32 us
    all_gather x1, blocking collectives, local(): lax.all_gather(pooled.reshape(N_DP * 8, HALF + META), 'core', axis=0)  5.82 us
    pallas_call x1, Pallas kernels, local(): pl.pallas_call(rows_kernel, out_shape=shape((1, ROWS, D), BF16), in_specs...  4.02 us
    all_gather x1, blocking collectives, local(): grads = lax.all_gather(grads.reshape(N_DP * 8, HALF), 'core', axis=0)  3.99 us
  transfers between devices with their start and end apart: 1, of which 1 were waited for; matrix products, arithmetic and copies ran while one was open for 0% of the time, Pallas kernels for 0%

profile of v1, /device:TPU:1, one launch (start us, length us, event | category | flops | bytes accessed | tf_op | source)
XLA Modules:
  0.0 120.9 jit_solution(7775389694548151079)
XLA Ops:
  0.6 0.0 copy-start
  0.6 1.6 %copy-done = bf16[1,256,4096]{2,1,0:T(8,128)(2,1)S(1)} copy-done((bf16[1,256,4096]{2,1,0:T(8,128)(2,1)S(1)}, bf16[1,256,4096]{2,1,0:T(8,128)(2,1)}, u32[]{:S(2)}) %copy-start) | copy-done | bytes 2097176
  2.2 0.0 copy-start.2
  2.2 0.7 copy-done.2
  2.9 0.0 copy-start.4
  2.9 0.7 copy-done.4
  3.6 0.0 copy-start.6
  3.6 0.7 copy-done.6
  4.3 2.9 %pool.1 = (bf16[12,8,2176]{2,1,0:T(8,128)(2,1)S(1)}, f32[8,256]{1,0:T(8,128)S(1)}) custom-call(bf16[1,256,4096]{2,1,0:T(8,128)(2,1)S(1)} %copy-done, s32[1,1,256]{2,1,0:T(1,128)S(1)} %copy-done.4, s32[1,4]{1,0:T(1,128)S(1)} %copy-done.6, f32[1,4096]{1,0:T(1,128)S(1)} %bitcast.8), custom_call_target="tpu_custom_call" | custom-call | tf_op jit(solution)/shard_map/pool/pallas_call | solution.py:205
  7.2 34.8 %all_to_all.15 = bf16[12,8,2176]{2,1,0:T(8,128)(2,1)S(1)} all-to-all(bf16[12,8,2176]{2,1,0:T(8,128)(2,1)S(1)} %get-tuple-element.9), channel_id=1, replica_groups=mesh['x'=4,'y'=8,'core'=2,'dp'=12] {'dp'}, dimensions={0} | all-to-all | bytes 835584 | tf_op jit(solution)/shard_map/pooled_exchange/all_to_all | solution.py:214
  41.9 0.0 copy-start.8
  41.9 5.8 %all_gather.12.pooled_ref = bf16[2,96,2176]{2,1,0:T(8,128)(2,1)S(1)} all-gather(bf16[1,96,2176]{2,1,0:T(8,128)(2,1)S(1)} %bitcast.10), channel_id=1, replica_groups=mesh['x'=4,'y'=8,'core'=2,'dp'=12] {'core'}, dimensions={0}, use_global_device_ids=true | all-gather | bytes 1253376 | tf_op jit(solution)/shard_map/pooled_exchange/all_gather | solution.py:215
  47.8 1.4 %unit.1 = (bf16[32,8,2048]{2,1,0:T(8,128)(2,1)}, f32[8,2048]{1,0:T(8,128)S(1)}, f32[8,128]{1,0:T(8,128)S(1)}) custom-call(bf16[2,96,2176]{2,1,0:T(8,128)(2,1)S(1)} %all_gather.12.pooled_ref), custom_call_target="tpu_custom_call" | custom-call | tf_op jit(solution)/shard_map/unit/pallas_call | solution.py:217
  49.2 9.7 %all-to-all-start.1 = ((bf16[32,8,2048]{2,1,0:T(8,128)(2,1)}), bf16[32,8,2048]{2,1,0:T(8,128)(2,1)S(1)}, u32[]{:S(2)}, u32[]{:S(2)}) async-start(bf16[32,8,2048]{2,1,0:T(8,128)(2,1)} %get-tuple-element.10), calls=%async_computation.1 | async-start | bytes 2097152 | tf_op jit(solution)/shard_map/unit_exchange/all_to_all | solution.py:225
  58.9 0.0 copy-done.8
  58.9 0.1 copy.8.positive_ref
  59.0 25.1 %all-to-all-done.1 = bf16[32,8,2048]{2,1,0:T(8,128)(2,1)S(1)} async-done(((bf16[32,8,2048]{2,1,0:T(8,128)(2,1)}), bf16[32,8,2048]{2,1,0:T(8,128)(2,1)S(1)}, u32[]{:S(2)}, u32[]{:S(2)}) %all-to-all-start.1) | async-done | bytes 1048608 | tf_op jit(solution)/shard_map/unit_exchange/all_to_all | solution.py:225
  84.1 0.7 gram.1
  84.8 0.0 copy-start.1
  84.8 0.0 copy-start.3
  84.8 0.0 copy-start.5
  84.8 0.0 copy-start.7
  84.8 6.3 %all-gather = f32[528,256]{1,0:T(8,128)S(1)} all-gather(f32[264,256]{1,0:T(8,128)S(1)} %gram.1), channel_id=2, replica_groups=mesh['x'=4,'y'=8,'core'=2,'dp'=12] {'core'}, dimensions={0}, use_global_device_ids=true | all-gather | bytes 811008 | tf_op jit(solution)/shard_map/gram/all_gather | solution.py:234
  91.2 0.8 contrast.1
  92.0 20.9 %all_to_all.16 = bf16[12,8,2048]{2,1,0:T(8,128)(2,1)S(1)} all-to-all(bf16[12,8,2048]{2,1,0:T(8,128)(2,1)S(1)} %get-tuple-element.14), channel_id=1, replica_groups=mesh['x'=4,'y'=8,'core'=2,'dp'=12] {'dp'}, dimensions={0} | all-to-all | bytes 786432 | tf_op jit(solution)/shard_map/grad_exchange/all_to_all | solution.py:244
  112.9 4.0 %all_gather.15.grad_ref = bf16[2,96,2048]{2,1,0:T(8,128)(2,1)S(1)} all-gather(bf16[1,96,2048]{2,1,0:T(8,128)(2,1)S(1)} %bitcast.11), channel_id=1, replica_groups=mesh['x'=4,'y'=8,'core'=2,'dp'=12] {'core'}, dimensions={0}, use_global_device_ids=true | all-gather | bytes 1179648 | tf_op jit(solution)/shard_map/grad_exchange/all_gather | solution.py:245
  116.9 0.0 copy-done.1
  116.9 0.0 copy-done.3
  116.9 0.0 copy-done.5
  116.9 0.0 copy-done.7
  116.9 4.0 %rows.1 = bf16[1,256,4096]{2,1,0:T(8,128)(2,1)} custom-call(bf16[2,96,2048]{2,1,0:T(8,128)(2,1)S(1)} %all_gather.15.grad_ref, bf16[1,256,4096]{2,1,0:T(8,128)(2,1)S(1)} %copy-done.1, s32[1,1,256]{2,1,0:T(1,128)S(1)} %copy-done.5, s32[1,4]{1,0:T(1,128)S(1)} %copy-done.7, f32[1,4096]{1,0:T(1,128)S(1)} %bitcast.9, f32[8,256]{1,0:T(8,128)S(1)} %get-tuple-element.15.inverse_ref), custom_call_target="tpu_custom_call" | custom-call | tf_op jit(solution)/shard_map/rows/pallas_call | solution.py:247
Async XLA Ops:
  0.6 1.6 %copy-start = (bf16[1,256,4096]{2,1,0:T(8,128)(2,1)S(1)}, bf16[1,256,4096]{2,1,0:T(8,128)(2,1)}, u32[]{:S(2)}) copy-start(bf16[1,256,4096]{2,1,0:T(8,128)(2,1)} %hidden_ref.3) | copy-start | bytes 6291460
  2.2 0.7 copy-start.2
  2.9 0.7 copy-start.4
  3.6 0.7 copy-start.6
  41.9 16.9 %copy-start.8 = (s32[64,4]{0,1:T(4,128)S(1)}, s32[64,4]{0,1:T(4,128)}, u32[]{:S(2)}) copy-start(s32[64,4]{0,1:T(4,128)} %param.8) | copy-start | bytes 3076
  49.2 34.9 %all-to-all-start.1 = ((bf16[32,8,2048]{2,1,0:T(8,128)(2,1)}), bf16[32,8,2048]{2,1,0:T(8,128)(2,1)S(1)}, u32[]{:S(2)}, u32[]{:S(2)}) async-start(bf16[32,8,2048]{2,1,0:T(8,128)(2,1)} %get-tuple-element.10), calls=%async_computation.1 | async-start | bytes 2097152 | tf_op jit(solution)/shard_map/unit_exchange/all_to_all | solution.py:225
  84.8 32.1 %copy-start.1 = (bf16[1,256,4096]{2,1,0:T(8,128)(2,1)S(1)}, bf16[1,256,4096]{2,1,0:T(8,128)(2,1)}, u32[]{:S(2)}) copy-start(bf16[1,256,4096]{2,1,0:T(8,128)(2,1)} %hidden_ref.3) | copy-start | bytes 6291460
  84.8 32.1 %copy-start.3 = (f32[4096]{0:T(1024)S(1)}, f32[4096]{0:T(1024)}, u32[]{:S(2)}) copy-start(f32[4096]{0:T(1024)} %param.9) | copy-start | bytes 49156
  84.8 32.1 %copy-start.5 = (s32[1,1,256]{2,1,0:T(1,128)S(1)}, s32[1,1,256]{2,1,0:T(1,128)}, u32[]{:S(2)}) copy-start(s32[1,1,256]{2,1,0:T(1,128)} %segment_ref.3) | copy-start | bytes 3076
  84.8 32.0 %copy-start.7 = (s32[1,4]{1,0:T(1,128)S(1)}, s32[1,4]{1,0:T(1,128)}, u32[]{:S(2)}) copy-start(s32[1,4]{1,0:T(1,128)} %assign_ref.3) | copy-start | bytes 52

commit v2 on v1

--- a/solution.py
+++ b/solution.py
@@ -18,13 +18,14 @@
 D = 4096
 HALF = D // 2
 PAS = 4
-META = 128
+CHUNK = 64
 N_DP = 12
 N_XY = 32
 BATCH = 256
 
 VMEM = pl.BlockSpec(memory_space=pltpu.VMEM)
 SMEM = pl.BlockSpec(memory_space=pltpu.SMEM)
+HBM = pl.BlockSpec(memory_space=pltpu.HBM)
 PARAMS = pltpu.CompilerParams(vmem_limit_bytes=40 * 1024 * 1024)
 
 
@@ -44,51 +45,81 @@
     return values[0:8] + values[8:16] + values[16:24]
 
 
-def pool_kernel(hidden_ref, segment_ref, assign_ref, gain_ref, send_ref, inverse_ref, squares):
-    def block(at, carry):
-        rows = pl.ds(pl.multiple_of(at * 16, 16), 16)
-        values = hidden_ref[0, rows, :].astype(F32)
-        total = jnp.sum(values * values, axis=1, keepdims=True)
-        squares[rows, :] = jnp.broadcast_to(total, (16, 128))
-        return carry
-
-    lax.fori_loop(0, ROWS // 16, block, 0)
-    inverse = lax.rsqrt(squares[...].T[0:8] * (1.0 / D) + norm_eps)
-    inverse_ref[...] = inverse
-    segment = jnp.broadcast_to(segment_ref[0], (8, ROWS))
+def pool_kernel(
+    hidden_hbm, segment_hbm, assign_hbm, gain_hbm, positive_hbm,
+    send_ref, upright_ref, partner_ref,
+    hidden, segment_at, assign_at, gain, positive, squares, chunk_sem, small_sem,
+):
+    chunks = [pl.ds(at * CHUNK, CHUNK) for at in range(ROWS // CHUNK)]
+    copies = [
+        pltpu.make_async_copy(hidden_hbm.at[0, rows], hidden.at[rows], chunk_sem.at[at])
+        for at, rows in enumerate(chunks)
+    ]
+    small = [
+        pltpu.make_async_copy(source, target, small_sem.at[at])
+        for at, (source, target) in enumerate(
+            [(segment_hbm, segment_at), (assign_hbm, assign_at), (positive_hbm, positive), (gain_hbm, gain)]
+        )
+    ]
+    copies[0].start()
+    for copy in small:
+        copy.start()
+    for copy in copies[1:]:
+        copy.start()
+
+    for copy in small:
+        copy.wait()
+    segment = jnp.broadcast_to(segment_at[0], (8, ROWS))
     onehot = jnp.where(segment == iota((8, ROWS), 0), 1.0, 0.0)
     counts = jnp.maximum(jnp.sum(onehot, axis=1, keepdims=True), 1.0)
+    row = iota((N_DP * 8, 8), 0)
+    lane = iota((N_DP * 8, 8), 1)
+    owner = jnp.zeros((N_DP * 8, 8), jnp.int32)
+    for k in range(PAS):
+        owner = jnp.where(lax.rem(lane, PAS) == k, assign_at[0:1, k : k + 1], owner)
+    slot = lax.div(row, 8) * PAS + lax.rem(row, PAS)
+    place = (owner == slot) & (lax.div(lax.rem(row, 8), PAS) == lax.div(lane, PAS))
+    place = jnp.where(place, 1.0, 0.0).astype(BF16)
+    lane = iota((64, BATCH), 1)
+    spread = jnp.where(lax.div(lane, PAS) == iota((64, BATCH), 0), 1.0, 0.0).astype(BF16)
+    partner = jnp.concatenate([positive[...].astype(F32), jnp.zeros((PAS, 64), F32)], axis=0)
+    partner = jnp.dot(partner.astype(BF16), spread, preferred_element_type=F32)
+    partner = jnp.where(lax.rem(iota((8, BATCH), 1), PAS) == iota((8, BATCH), 0), partner, 0.0)
+    partner_ref[...] = jnp.sum(partner, axis=0, keepdims=True).astype(jnp.int32)
+
+    for at in range(ROWS // CHUNK):
+        copies[at].wait()
+
+        def block(step, carry):
+            rows = pl.ds(pl.multiple_of(at * CHUNK + step * 16, 16), 16)
+            values = hidden[rows, :].astype(F32)
+            total = jnp.sum(values * values, axis=1, keepdims=True)
+            squares[rows, :] = jnp.broadcast_to(total, (16, 128))
+            return carry
+
+        lax.fori_loop(0, CHUNK // 16, block, 0)
+    inverse = lax.rsqrt(squares[...].T[0:8] * (1.0 / D) + norm_eps)
     weights = split3(onehot * inverse)
-    slot = iota((8, META), 0)
-    meta = jnp.zeros((8, META), F32)
-    for k in range(PAS):
-        meta = jnp.where(lax.rem(slot, PAS) == k, assign_ref[0, k].astype(F32), meta)
-    lane = lax.axis_index("dp") * 8 + slot
-    meta = jnp.where(iota((8, META), 1) == lane, meta, 0.0).astype(BF16)
     halves = []
     for h in range(2):
         columns = pl.ds(h * HALF, HALF)
-        pooled = sum3(jnp.dot(weights, hidden_ref[0, :, columns], preferred_element_type=F32))
-        halves.append((pooled * gain_ref[:, columns] / counts)[0:PAS])
+        pooled = sum3(jnp.dot(weights, hidden[:, columns], preferred_element_type=F32))
+        halves.append((pooled * gain[:, columns] / counts)[0:PAS])
     packed = jnp.concatenate(halves, axis=0).astype(BF16)
-    for peer in range(N_DP):
-        send_ref[peer, :, 0:HALF] = packed
-        send_ref[peer, :, HALF:] = meta
+    placed = jnp.dot(place, packed, preferred_element_type=F32).astype(BF16)
+    send_ref[...] = placed.reshape(N_DP, 8, HALF)
+    upright_ref[...] = jnp.concatenate(
+        [onehot, onehot, onehot, inverse, jnp.zeros((96, ROWS), F32)], axis=0
+    ).T
 
 
 def unit_kernel(pooled_ref, send_ref, embed_ref, length_ref):
     core = lax.axis_index("core")
-    wanted = lax.axis_index("dp") * PAS
-    row = iota((8, META), 0)
-    lane = iota((8, META), 1)
     embeds, lengths = [], []
     for c in range(2):
-        owners = jnp.sum(pooled_ref[c, :, HALF:].astype(F32), axis=0, keepdims=True)
-        hit = (owners == (wanted + lax.rem(row, PAS)).astype(F32)) & (
-            lax.div(lax.rem(lane, 8), PAS) == lax.div(row, PAS)
-        )
-        select = jnp.where(hit & (lane < N_DP * 8), 1.0, 0.0)[:, : N_DP * 8].astype(BF16)
-        embed = jnp.dot(select, pooled_ref[c, :, 0:HALF], preferred_element_type=F32)
+        embed = pooled_ref[c, 0].astype(F32)
+        for peer in range(1, N_DP):
+            embed = embed + pooled_ref[c, peer].astype(F32)
         squares = jnp.sum(embed * embed, axis=1, keepdims=True)
         squares = squares[0:PAS] + squares[PAS:]
         embeds.append(embed)
@@ -115,19 +146,14 @@
     )
 
 
-def contrast_kernel(gram_ref, unit_ref, embed_ref, length_ref, positive_ref, loss_ref, send_ref):
+def contrast_kernel(gram_ref, unit_ref, embed_ref, length_ref, partner_ref, loss_ref, send_ref):
     core = lax.axis_index("core")
     first = (lax.axis_index("x") * 8 + lax.axis_index("y")) * 8
     shift = inv_tau
     row = iota((8, BATCH), 0)
     lane = iota((8, BATCH), 1)
     mine = first + row
-    lanes = iota((64, BATCH), 1)
-    partner = jnp.zeros((64, BATCH), jnp.int32)
-    for s in range(PAS):
-        partner = jnp.where(lax.rem(lanes, PAS) == s, positive_ref[:, s : s + 1], partner)
-    partner = jnp.where(lax.div(lanes, PAS) == iota((64, BATCH), 0), partner, 0)
-    partner = jnp.sum(partner, axis=0, keepdims=True)
+    partner = partner_ref[...]
     own_partner = jnp.sum(jnp.where(lane == mine, partner, 0), axis=1, keepdims=True)
 
     logits = (gram_ref[0, 0:BATCH] + gram_ref[1, 0:BATCH]) * inv_tau
@@ -158,7 +184,8 @@
 
 
 def rows_kernel(
-    grad_ref, hidden_ref, segment_ref, assign_ref, gain_ref, inverse_ref, out_ref, scaled, coef
+    grad_ref, hidden_ref, segment_ref, assign_ref, gain_ref, upright_ref, out_hbm,
+    scaled, coef, out, sems,
 ):
     core = lax.axis_index("core")
     row = iota((8, N_DP * 8), 0)
@@ -176,9 +203,7 @@
         columns = pl.ds(h * HALF, HALF)
         part = jnp.dot(select, grad_ref[h], preferred_element_type=F32)
         scaled[:, columns] = split3(gain_ref[:, columns] * (part / counts))
-    upright = jnp.concatenate(
-        [onehot, onehot, onehot, inverse_ref[...], jnp.zeros((96, ROWS), F32)], axis=0
-    ).T
+    upright = upright_ref[...]
     spread = upright[:, 0:24]
     inverse = upright[:, 24:25]
     dots = lax.dot_general(
@@ -189,30 +214,48 @@
     coef[:, 128:256] = jnp.broadcast_to(inverse * inverse * inverse * dot, (ROWS, 128))
     spread = spread.astype(BF16)
     width = 512
+    copies = []
     for at in range(0, D, width):
         columns = pl.ds(at, width)
         gained = jnp.dot(spread, scaled[:, columns], preferred_element_type=F32)
         values = hidden_ref[0, :, columns].astype(F32)
-        out_ref[0, :, columns] = (
-            coef[:, 0:1] * gained - values * coef[:, 128:129]
-        ).astype(BF16)
+        out[:, columns] = (coef[:, 0:1] * gained - values * coef[:, 128:129]).astype(BF16)
+        copy = pltpu.make_async_copy(
+            out.at[:, columns], out_hbm.at[0, :, columns], sems.at[at // width]
+        )
+        copy.start()
+        copies.append(copy)
+    for copy in copies:
+        copy.wait()
 
 
 def local(hidden, segment_ids, assign, positive, gain):
     shape = jax.ShapeDtypeStruct
     gain = gain.reshape(1, D)
     with jax.named_scope("pool"):
-        send, inverse = pl.pallas_call(
+        send, upright, partner = pl.pallas_call(
             pool_kernel,
-            out_shape=(shape((N_DP, 8, HALF + META), BF16), shape((8, ROWS), F32)),
-            in_specs=[VMEM, VMEM, SMEM, VMEM],
-            out_specs=(VMEM, VMEM),
-            scratch_shapes=[pltpu.VMEM((ROWS, 128), F32)],
-            compiler_params=PARAMS,
-        )(hidden, segment_ids, assign, gain)
+            out_shape=(
+                shape((N_DP, 8, HALF), BF16),
+                shape((ROWS, 128), F32),
+                shape((1, BATCH), jnp.int32),
+            ),
+            in_specs=[HBM] * 5,
+            out_specs=(VMEM, VMEM, VMEM),
+            scratch_shapes=[
+                pltpu.VMEM((ROWS, D), BF16),
+                pltpu.VMEM((1, 1, ROWS), jnp.int32),
+                pltpu.VMEM((1, PAS), jnp.int32),
+                pltpu.VMEM((1, D), F32),
+                pltpu.VMEM((PAS, 64), jnp.int32),
+                pltpu.VMEM((ROWS, 128), F32),
+                pltpu.SemaphoreType.DMA((ROWS // CHUNK,)),
+                pltpu.SemaphoreType.DMA((4,)),
+            ],
+            compiler_params=PARAMS,
+        )(*[pltpu.with_memory_space_constraint(v, pltpu.HBM) for v in (hidden, segment_ids, assign, gain, positive.T)])
     with jax.named_scope("pooled_exchange"):
-        pooled = lax.all_to_all(send, "dp", 0, 0)
-        pooled = lax.all_gather(pooled.reshape(N_DP * 8, HALF + META), "core", axis=0)
+        pooled = lax.all_gather(lax.all_to_all(send, "dp", 0, 0), "core", axis=0)
     with jax.named_scope("unit"):
         send, embed, length = pl.pallas_call(
             unit_kernel,
@@ -239,7 +282,7 @@
             in_specs=[VMEM] * 5,
             out_specs=(VMEM, VMEM),
             compiler_params=PARAMS,
-        )(gram, units, embed, length, positive)
+        )(gram, units, embed, length, partner)
     with jax.named_scope("grad_exchange"):
         grads = lax.all_to_all(send, "dp", 0, 0)
         grads = lax.all_gather(grads.reshape(N_DP * 8, HALF), "core", axis=0)
@@ -248,10 +291,15 @@
             rows_kernel,
             out_shape=shape((1, ROWS, D), BF16),
             in_specs=[VMEM, VMEM, VMEM, SMEM, VMEM, VMEM],
-            out_specs=VMEM,
-            scratch_shapes=[pltpu.VMEM((24, D), BF16), pltpu.VMEM((ROWS, 256), F32)],
-            compiler_params=PARAMS,
-        )(grads, hidden, segment_ids, assign, gain, inverse)
+            out_specs=HBM,
+            scratch_shapes=[
+                pltpu.VMEM((24, D), BF16),
+                pltpu.VMEM((ROWS, 256), F32),
+                pltpu.VMEM((ROWS, D), BF16),
+                pltpu.SemaphoreType.DMA((8,)),
+            ],
+            compiler_params=PARAMS,
+        )(grads, hidden, segment_ids, assign, gain, upright)
     return loss, grad_rows
 
 

time: 121 us -> 116 us (0.959)
  blocking collectives: 71.8 us -> 105 us
  waiting for transfers between devices: 25.1 us -> 0 us
  starting transfers between devices: 9.67 us -> 0 us
  local copies, waits for them, and re-layouts: 3.76 us -> 0.03 us
    all_to_all x1 -> x2, blocking collectives: 34.8 us -> 68.9 us  [the longest x1 34.7 us: local(): units = lax.all_to_all(send, ('x', 'y'), 0, 0).reshape(BATCH, HALF)]
    all_to_all x1 -> x0, waiting for transfers between devices: 25.1 us -> none  [local(): units = lax.all_to_all(send, ('x', 'y'), 0, 0).reshape(BATCH, HALF)]
    all_to_all x1 -> x0, starting transfers between devices: 9.67 us -> none  [local(): units = lax.all_to_all(send, ('x', 'y'), 0, 0).reshape(BATCH, HALF)]
    unnamed x19 -> x8, local copies, waits for them, and re-layouts: 3.76 us -> 0.03 us
    all_gather x1, blocking collectives: 5.82 us -> 4.02 us  [local(): pooled = lax.all_gather(lax.all_to_all(send, 'dp', 0, 0), 'core', axis=0)]
  transfers between devices with their start and end apart: 1 -> 0, of which waited for: 1 -> 0; matrix products, arithmetic and copies ran while one was open for 0% -> 0% of each run, Pallas kernels for 0% -> 0%
where the time goes in v2:
time: 116 us; the launch traced here: 115 us
  blocking collectives  105 us (91%)
  Pallas kernels  9.85 us (8%)
    all_to_all x1, blocking collectives, local(): units = lax.all_to_all(send, ('x', 'y'), 0, 0).reshape(BATCH, HALF)  34.7 us
    all_to_all x1, blocking collectives, local(): pooled = lax.all_gather(lax.all_to_all(send, 'dp', 0, 0), 'core', axis=0)  34.2 us
    all_to_all x1, blocking collectives, local(): grads = lax.all_to_all(send, 'dp', 0, 0)  21.2 us
    all_gather x1, blocking collectives, local(): gram = lax.all_gather(gram, 'core', axis=0)  6.3 us
    all_gather x1, blocking collectives, local(): grads = lax.all_gather(grads.reshape(N_DP * 8, HALF), 'core', axis=0)  4.38 us
    pallas_call x1, Pallas kernels, local(): pl.pallas_call(rows_kernel, out_shape=shape((1, ROWS, D), BF16), in_specs...  4.05 us
    all_gather x1, blocking collectives, local(): pooled = lax.all_gather(lax.all_to_all(send, 'dp', 0, 0), 'core', axis=0)  4.02 us
    pallas_call x1, Pallas kernels, local(): pl.pallas_call(pool_kernel, out_shape=(shape((N_DP, 8, HALF), BF16), shap...  4 us

profile of v2, /device:TPU:1, one launch (start us, length us, event | category | flops | bytes accessed | tf_op | source)
XLA Modules:
  0.0 115.3 jit_solution(16824420995154867398)
XLA Ops:
  0.6 4.0 %pool.1 = (bf16[12,8,2048]{2,1,0:T(8,128)(2,1)S(1)}, f32[256,128]{1,0:T(8,128)S(1)}, s32[1,256]{1,0:T(1,128)S(1)}) custom-call(bf16[1,256,4096]{2,1,0:T(8,128)(2,1)} %hidden_ref.1, s32[1,1,256]{2,1,0:T(1,128)} %segment_ref.1, s32[1,4]{1,0:T(1,128)} %assign_ref.1, f32[1,4096]{1,0:T(1,128)} %bitcast.10, s32[4,64]{1,0:T(4,128)} %bitcast.13), custom_call_target="tpu_custom_call" | custom-call | tf_op jit(solution)/shard_map/pool/pallas_call | solution.py:236
  4.6 34.2 %all_to_all.15 = bf16[12,8,2048]{2,1,0:T(8,128)(2,1)S(1)} all-to-all(bf16[12,8,2048]{2,1,0:T(8,128)(2,1)S(1)} %get-tuple-element.10), channel_id=1, replica_groups=mesh['x'=4,'y'=8,'core'=2,'dp'=12] {'dp'}, dimensions={0} | all-to-all | bytes 786432 | tf_op jit(solution)/shard_map/pooled_exchange/all_to_all | solution.py:258
  38.8 4.0 %all-gather = bf16[24,8,2048]{2,1,0:T(8,128)(2,1)S(1)} all-gather(bf16[12,8,2048]{2,1,0:T(8,128)(2,1)S(1)} %all_to_all.15), channel_id=2, replica_groups=mesh['x'=4,'y'=8,'core'=2,'dp'=12] {'core'}, dimensions={0}, use_global_device_ids=true | all-gather | bytes 1179648 | tf_op jit(solution)/shard_map/pooled_exchange/all_gather | solution.py:258
  42.9 0.3 unit.1
  43.2 34.7 %all_to_all.16 = bf16[32,8,2048]{2,1,0:T(8,128)(2,1)S(1)} all-to-all(bf16[32,8,2048]{2,1,0:T(8,128)(2,1)S(1)} %get-tuple-element.11), channel_id=1, replica_groups=mesh['x'=4,'y'=8,'core'=2,'dp'=12] {'x','y'}, dimensions={0} | all-to-all | bytes 2097152 | tf_op jit(solution)/shard_map/unit_exchange/all_to_all | solution.py:268
  77.9 0.7 gram.1
  78.6 0.0 copy-start
  78.6 0.0 copy-start.1
  78.6 0.0 copy-start.2
  78.6 0.0 copy-start.3
  78.7 6.3 %all-gather.1 = f32[528,256]{1,0:T(8,128)S(1)} all-gather(f32[264,256]{1,0:T(8,128)S(1)} %gram.1), channel_id=3, replica_groups=mesh['x'=4,'y'=8,'core'=2,'dp'=12] {'core'}, dimensions={0}, use_global_device_ids=true | all-gather | bytes 811008 | tf_op jit(solution)/shard_map/gram/all_gather | solution.py:277
  85.0 0.7 contrast.1
  85.7 21.2 %all_to_all.17 = bf16[12,8,2048]{2,1,0:T(8,128)(2,1)S(1)} all-to-all(bf16[12,8,2048]{2,1,0:T(8,128)(2,1)S(1)} %get-tuple-element.16), channel_id=1, replica_groups=mesh['x'=4,'y'=8,'core'=2,'dp'=12] {'dp'}, dimensions={0} | all-to-all | bytes 786432 | tf_op jit(solution)/shard_map/grad_exchange/all_to_all | solution.py:287
  106.9 4.4 %all_gather.19.grad_ref = bf16[2,96,2048]{2,1,0:T(8,128)(2,1)S(1)} all-gather(bf16[1,96,2048]{2,1,0:T(8,128)(2,1)S(1)} %bitcast.12), channel_id=1, replica_groups=mesh['x'=4,'y'=8,'core'=2,'dp'=12] {'core'}, dimensions={0}, use_global_device_ids=true | all-gather | bytes 1179648 | tf_op jit(solution)/shard_map/grad_exchange/all_gather | solution.py:288
  111.2 0.0 copy-done
  111.2 0.0 copy-done.1
  111.3 0.0 copy-done.2
  111.3 0.0 copy-done.3
  111.3 4.1 %rows.1 = bf16[1,256,4096]{2,1,0:T(8,128)(2,1)} custom-call(bf16[2,96,2048]{2,1,0:T(8,128)(2,1)S(1)} %all_gather.19.grad_ref, bf16[1,256,4096]{2,1,0:T(8,128)(2,1)S(1)} %copy-done, s32[1,1,256]{2,1,0:T(1,128)S(1)} %copy-done.2, s32[1,4]{1,0:T(1,128)S(1)} %copy-done.3, f32[1,4096]{1,0:T(1,128)S(1)} %bitcast.11, f32[256,128]{1,0:T(8,128)S(1)} %get-tuple-element.17.upright_ref), custom_call_target="tpu_custom_call" | custom-call | tf_op jit(solution)/shard_map/rows/pallas_call | solution.py:290
Async XLA Ops:
  78.6 32.6 %copy-start = (bf16[1,256,4096]{2,1,0:T(8,128)(2,1)S(1)}, bf16[1,256,4096]{2,1,0:T(8,128)(2,1)}, u32[]{:S(2)}) copy-start(bf16[1,256,4096]{2,1,0:T(8,128)(2,1)} %hidden_ref.1) | copy-start | bytes 6291460
  78.6 32.6 %copy-start.1 = (f32[4096]{0:T(1024)S(1)}, f32[4096]{0:T(1024)}, u32[]{:S(2)}) copy-start(f32[4096]{0:T(1024)} %param.9) | copy-start | bytes 49156
  78.6 32.6 %copy-start.2 = (s32[1,1,256]{2,1,0:T(1,128)S(1)}, s32[1,1,256]{2,1,0:T(1,128)}, u32[]{:S(2)}) copy-start(s32[1,1,256]{2,1,0:T(1,128)} %segment_ref.1) | copy-start | bytes 3076
  78.6 32.6 %copy-start.3 = (s32[1,4]{1,0:T(1,128)S(1)}, s32[1,4]{1,0:T(1,128)}, u32[]{:S(2)}) copy-start(s32[1,4]{1,0:T(1,128)} %assign_ref.1) | copy-start | bytes 52

commit v3 on v2

--- a/solution.py
+++ b/solution.py
@@ -17,10 +17,12 @@
 ROWS = 256
 D = 4096
 HALF = D // 2
+QUARTER = D // 4
 PAS = 4
 CHUNK = 64
 N_DP = 12
-N_XY = 32
+N_X = 4
+N_Y = 8
 BATCH = 256
 
 VMEM = pl.BlockSpec(memory_space=pltpu.VMEM)
@@ -48,7 +50,7 @@
 def pool_kernel(
     hidden_hbm, segment_hbm, assign_hbm, gain_hbm, positive_hbm,
     send_ref, upright_ref, partner_ref,
-    hidden, segment_at, assign_at, gain, positive, squares, chunk_sem, small_sem,
+    hidden, segment_at, assign_at, gain, positive, sums, chunk_sem, small_sem,
 ):
     chunks = [pl.ds(at * CHUNK, CHUNK) for at in range(ROWS // CHUNK)]
     copies = [
@@ -94,59 +96,46 @@
             rows = pl.ds(pl.multiple_of(at * CHUNK + step * 16, 16), 16)
             values = hidden[rows, :].astype(F32)
             total = jnp.sum(values * values, axis=1, keepdims=True)
-            squares[rows, :] = jnp.broadcast_to(total, (16, 128))
+            sums[rows, :] = jnp.broadcast_to(total, (16, 128))
             return carry
 
         lax.fori_loop(0, CHUNK // 16, block, 0)
-    inverse = lax.rsqrt(squares[...].T[0:8] * (1.0 / D) + norm_eps)
+    inverse = lax.rsqrt(sums[...].T[0:8] * (1.0 / D) + norm_eps)
     weights = split3(onehot * inverse)
-    halves = []
     for h in range(2):
         columns = pl.ds(h * HALF, HALF)
         pooled = sum3(jnp.dot(weights, hidden[:, columns], preferred_element_type=F32))
-        halves.append((pooled * gain[:, columns] / counts)[0:PAS])
-    packed = jnp.concatenate(halves, axis=0).astype(BF16)
-    placed = jnp.dot(place, packed, preferred_element_type=F32).astype(BF16)
-    send_ref[...] = placed.reshape(N_DP, 8, HALF)
+        pooled = (pooled * gain[:, columns] / counts)[0:PAS]
+        pooled = jnp.concatenate([pooled[:, 0:QUARTER], pooled[:, QUARTER:]], axis=0).astype(BF16)
+        placed = jnp.dot(place, pooled, preferred_element_type=F32).astype(BF16)
+        send_ref[h] = placed.reshape(N_DP, 8, QUARTER)
     upright_ref[...] = jnp.concatenate(
         [onehot, onehot, onehot, inverse, jnp.zeros((96, ROWS), F32)], axis=0
     ).T
 
 
-def unit_kernel(pooled_ref, send_ref, embed_ref, length_ref):
-    core = lax.axis_index("core")
-    embeds, lengths = [], []
+def owned_kernel(pooled_ref, send_ref, embed_ref):
+    embeds = []
     for c in range(2):
         embed = pooled_ref[c, 0].astype(F32)
         for peer in range(1, N_DP):
             embed = embed + pooled_ref[c, peer].astype(F32)
-        squares = jnp.sum(embed * embed, axis=1, keepdims=True)
-        squares = squares[0:PAS] + squares[PAS:]
-        embeds.append(embed)
-        lengths.append(jnp.sqrt(squares + norm_eps))
-    length = jnp.concatenate(lengths, axis=0)
-    own = jnp.where(
-        core == 0,
-        jnp.concatenate([embeds[0][0:PAS], embeds[1][0:PAS]], axis=0),
-        jnp.concatenate([embeds[0][PAS:], embeds[1][PAS:]], axis=0),
+        embeds.append(jnp.concatenate([embed[0:PAS], embed[PAS:]], axis=1))
+    own = jnp.concatenate(embeds, axis=0)
+    embed_ref[...] = own
+    own = own.astype(BF16)
+    for peer in range(N_Y):
+        send_ref[peer] = own
+
+
+def gram_kernel(embed_ref, gram_ref):
+    embeds = embed_ref[...]
+    gram_ref[...] = lax.dot_general(
+        embeds, embeds, (((1,), (1,)), ((), ())), preferred_element_type=F32
     )
-    embed_ref[...] = own
-    length_ref[...] = jnp.broadcast_to(length, (8, 128))
-    unit = (own / length).astype(BF16)
-    for peer in range(N_XY):
-        send_ref[peer] = unit
-
-
-def gram_kernel(unit_ref, embed_ref, gram_ref):
-    units = unit_ref[...]
-    dims = (((1,), (1,)), ((), ()))
-    gram_ref[0:BATCH] = lax.dot_general(units, units, dims, preferred_element_type=F32)
-    gram_ref[BATCH:] = lax.dot_general(
-        embed_ref[...].astype(BF16), units, dims, preferred_element_type=F32
-    )
-
-
-def contrast_kernel(gram_ref, unit_ref, embed_ref, length_ref, partner_ref, loss_ref, send_ref):
+
+
+def contrast_kernel(gram_ref, batch_ref, embed_ref, partner_ref, loss_ref, send_ref):
     core = lax.axis_index("core")
     first = (lax.axis_index("x") * 8 + lax.axis_index("y")) * 8
     shift = inv_tau
@@ -156,28 +145,34 @@
     partner = partner_ref[...]
     own_partner = jnp.sum(jnp.where(lane == mine, partner, 0), axis=1, keepdims=True)
 
-    logits = (gram_ref[0, 0:BATCH] + gram_ref[1, 0:BATCH]) * inv_tau
+    gram = gram_ref[0] + gram_ref[1]
     everyone = iota((BATCH, BATCH), 0) == iota((BATCH, BATCH), 1)
-    logits = jnp.where(everyone, -1e30, logits)
+    diagonal = jnp.where(everyone, gram, 0.0)
+    across = lax.rsqrt(jnp.sum(diagonal, axis=0, keepdims=True) + norm_eps)
+    down = lax.rsqrt(jnp.sum(diagonal, axis=1, keepdims=True) + norm_eps)
+    logits = jnp.where(everyone, -1e30, gram * down * across * inv_tau)
     lse_all = shift + jnp.log(jnp.sum(jnp.exp(logits - shift), axis=0, keepdims=True))
     at = pl.ds(pl.multiple_of(first, 8), 8)
-    own = (gram_ref[0, at, :] + gram_ref[1, at, :]) * inv_tau
-    own = jnp.where(lane == mine, -1e30, own)
+    own = gram_ref[0, at, :] + gram_ref[1, at, :]
+    scale = lax.rsqrt(
+        jnp.sum(jnp.where(lane == mine, own, 0.0), axis=1, keepdims=True) + norm_eps
+    )
+    cosine = own * scale * across
+    own = jnp.where(lane == mine, -1e30, cosine * inv_tau)
     lse = shift + jnp.log(jnp.sum(jnp.exp(own - shift), axis=1, keepdims=True))
     hits = lane == own_partner
     loss = lse - jnp.sum(jnp.where(hits, own, 0.0), axis=1, keepdims=True)
     as_query = loss_scale * (jnp.exp(own - lse) - jnp.where(hits, 1.0, 0.0))
     as_key = loss_scale * (jnp.exp(own - lse_all) - jnp.where(partner == mine, 1.0, 0.0))
-    weights = jnp.concatenate([as_query, as_key], axis=0).astype(BF16)
-    grad = jnp.dot(weights, unit_ref[...], preferred_element_type=F32)
-    grad = (grad[0:8] + grad[8:16]) * inv_tau
-    weights = weights.astype(F32)
-    length = length_ref[:, 0:1]
-    along = (gram_ref[0, BATCH:] + gram_ref[1, BATCH:]) / length
-    inner = inv_tau * jnp.sum((weights[0:8] + weights[8:16]) * along, axis=1, keepdims=True)
-    grad = ((grad - embed_ref[...] / length * inner) / length).astype(BF16)
-    for peer in range(N_DP):
-        send_ref[peer] = grad
+    weights = as_query.astype(BF16).astype(F32) + as_key.astype(BF16).astype(F32)
+    inner = inv_tau * jnp.sum(weights * cosine, axis=1, keepdims=True)
+    grad = jnp.dot(split3(weights * across), batch_ref[...], preferred_element_type=F32)
+    grad = (sum3(grad) * inv_tau - embed_ref[...] * (scale * inner)) * scale
+    for c in range(2):
+        part = grad[c * PAS : (c + 1) * PAS]
+        part = jnp.concatenate([part[:, 0:QUARTER], part[:, QUARTER:]], axis=0).astype(BF16)
+        for peer in range(N_DP):
+            send_ref[c, peer] = part
     place = (iota((8, 128), 1) + core * PAS) == iota((8, 128), 0)
     loss = jnp.sum(jnp.where(place, loss, 0.0), axis=0, keepdims=True)
     loss_ref[...] = loss[:, 0:PAS]
@@ -187,22 +182,23 @@
     grad_ref, hidden_ref, segment_ref, assign_ref, gain_ref, upright_ref, out_hbm,
     scaled, coef, out, sems,
 ):
-    core = lax.axis_index("core")
     row = iota((8, N_DP * 8), 0)
     lane = iota((8, N_DP * 8), 1)
     select = jnp.zeros((8, N_DP * 8), F32)
     for k in range(PAS):
         owner = assign_ref[0, k]
-        at = lax.div(owner, PAS) * 8 + core * PAS + lax.rem(owner, PAS)
-        select = jnp.where((row == k) & (lane == at), 1.0, select)
+        at = lax.div(owner, PAS) * 8 + lax.rem(owner, PAS) + lax.div(row, PAS) * PAS
+        select = jnp.where((lax.rem(row, PAS) == k) & (lane == at), 1.0, select)
     select = select.astype(BF16)
     segment = jnp.broadcast_to(segment_ref[0], (8, ROWS))
     onehot = jnp.where(segment == iota((8, ROWS), 0), 1.0, 0.0)
     counts = jnp.maximum(jnp.sum(onehot, axis=1, keepdims=True), 1.0)
     for h in range(2):
-        columns = pl.ds(h * HALF, HALF)
         part = jnp.dot(select, grad_ref[h], preferred_element_type=F32)
-        scaled[:, columns] = split3(gain_ref[:, columns] * (part / counts))
+        for q in range(2):
+            columns = pl.ds((h * 2 + q) * QUARTER, QUARTER)
+            scaled[:, columns] = split3(gain_ref[:, columns] * (part / counts))
+            part = jnp.concatenate([part[PAS:], part[0:PAS]], axis=0)
     upright = upright_ref[...]
     spread = upright[:, 0:24]
     inverse = upright[:, 24:25]
@@ -236,7 +232,7 @@
         send, upright, partner = pl.pallas_call(
             pool_kernel,
             out_shape=(
-                shape((N_DP, 8, HALF), BF16),
+                shape((2, N_DP, 8, QUARTER), BF16),
                 shape((ROWS, 128), F32),
                 shape((1, BATCH), jnp.int32),
             ),
@@ -255,37 +251,40 @@
             compiler_params=PARAMS,
         )(*[pltpu.with_memory_space_constraint(v, pltpu.HBM) for v in (hidden, segment_ids, assign, gain, positive.T)])
     with jax.named_scope("pooled_exchange"):
-        pooled = lax.all_gather(lax.all_to_all(send, "dp", 0, 0), "core", axis=0)
-    with jax.named_scope("unit"):
-        send, embed, length = pl.pallas_call(
-            unit_kernel,
-            out_shape=(shape((N_XY, 8, HALF), BF16), shape((8, HALF), F32), shape((8, 128), F32)),
+        pooled = lax.all_to_all(send.reshape(2 * N_DP, 8, -1), ("core", "dp"), 0, 0)
+        pooled = pooled.reshape(2, N_DP, 8, -1)
+    with jax.named_scope("owned"):
+        send, embed = pl.pallas_call(
+            owned_kernel,
+            out_shape=(shape((N_Y, 8, HALF), BF16), shape((8, HALF), F32)),
             in_specs=[VMEM],
-            out_specs=(VMEM, VMEM, VMEM),
+            out_specs=(VMEM, VMEM),
             compiler_params=PARAMS,
         )(pooled)
-    with jax.named_scope("unit_exchange"):
-        units = lax.all_to_all(send, ("x", "y"), 0, 0).reshape(BATCH, HALF)
+    with jax.named_scope("embed_exchange"):
+        batch = lax.all_to_all(send, "y", 0, 0).reshape(N_Y * 8, HALF)
+        batch = jnp.broadcast_to(batch, (N_X, N_Y * 8, HALF))
+        batch = lax.all_to_all(batch, "x", 0, 0).reshape(BATCH, HALF)
     with jax.named_scope("gram"):
         gram = pl.pallas_call(
             gram_kernel,
-            out_shape=shape((BATCH + 8, BATCH), F32),
-            in_specs=[VMEM, VMEM],
+            out_shape=shape((BATCH, BATCH), F32),
+            in_specs=[VMEM],
             out_specs=VMEM,
             compiler_params=PARAMS,
-        )(units, embed)
+        )(batch)
         gram = lax.all_gather(gram, "core", axis=0)
     with jax.named_scope("contrast"):
         loss, send = pl.pallas_call(
             contrast_kernel,
-            out_shape=(shape((1, PAS), F32), shape((N_DP, 8, HALF), BF16)),
-            in_specs=[VMEM] * 5,
+            out_shape=(shape((1, PAS), F32), shape((2, N_DP, 8, QUARTER), BF16)),
+            in_specs=[VMEM] * 4,
             out_specs=(VMEM, VMEM),
             compiler_params=PARAMS,
-        )(gram, units, embed, length, partner)
+        )(gram, batch, embed, partner)
     with jax.named_scope("grad_exchange"):
-        grads = lax.all_to_all(send, "dp", 0, 0)
-        grads = lax.all_gather(grads.reshape(N_DP * 8, HALF), "core", axis=0)
+        grads = lax.all_to_all(send.reshape(2 * N_DP, 8, QUARTER), ("core", "dp"), 0, 0)
+        grads = grads.reshape(2, N_DP * 8, QUARTER)
     with jax.named_scope("rows"):
         grad_rows = pl.pallas_call(
             rows_kernel,

time: 116 us -> 111 us (0.957)
  blocking collectives: 105 us -> 100 us
    all_gather x2 -> x0, blocking collectives: 8.4 us -> none  [the longest x1 4.38 us: local(): grads = lax.all_gather(grads.reshape(N_DP * 8, HALF), 'core', axis=0)]
    all_to_all x3 -> x4, blocking collectives: 90 us -> 96.5 us  [the longest x1 36.4 us: local(): pooled = lax.all_to_all(send.reshape(2 * N_DP, 8, -1), ('core', 'dp'), 0, 0)]
    all_gather x1, blocking collectives: 6.3 us -> 3.78 us  [local(): gram = lax.all_gather(gram, 'core', axis=0)]
where the time goes in v3:
time: 111 us
  blocking collectives  100 us (90%)
  Pallas kernels  9.5 us (9%)
    all_to_all x1, blocking collectives, local(): pooled = lax.all_to_all(send.reshape(2 * N_DP, 8, -1), ('core', 'dp'), 0, 0)  36.4 us
    all_to_all x1, blocking collectives, local(): lax.all_to_all(send.reshape(2 * N_DP, 8, QUARTER), ('core', 'dp'), 0, 0)  23 us
    all_to_all x1, blocking collectives, local(): batch = lax.all_to_all(send, 'y', 0, 0).reshape(N_Y * 8, HALF)  19 us
    all_to_all x1, blocking collectives, local(): batch = lax.all_to_all(batch, 'x', 0, 0).reshape(BATCH, HALF)  18 us
    pallas_call x1, Pallas kernels, local(): pl.pallas_call(pool_kernel, out_shape=(shape((2, N_DP, 8, QUARTER), BF16)...  4.09 us
    pallas_call x1, Pallas kernels, local(): pl.pallas_call(rows_kernel, out_shape=shape((1, ROWS, D), BF16), in_specs...  4.04 us
    all_gather x1, blocking collectives, local(): gram = lax.all_gather(gram, 'core', axis=0)  3.78 us

profile of v3, /device:TPU:1, one launch (start us, length us, event | category | flops | bytes accessed | tf_op | source)
XLA Modules:
  0.0 110.5 jit_solution(2854742680726974962)
XLA Ops:
  0.6 4.1 %pool.1 = (bf16[2,12,8,1024]{3,2,1,0:T(8,128)(2,1)S(1)}, f32[256,128]{1,0:T(8,128)S(1)}, s32[1,256]{1,0:T(1,128)S(1)}) custom-call(bf16[1,256,4096]{2,1,0:T(8,128)(2,1)} %hidden_ref.1, s32[1,1,256]{2,1,0:T(1,128)} %segment_ref.1, s32[1,4]{1,0:T(1,128)} %assign_ref.1, f32[1,4096]{1,0:T(1,128)} %bitcast.16, s32[4,64]{1,0:T(4,128)} %bitcast.19), custom_call_target="tpu_custom_call" | custom-call | tf_op jit(solution)/shard_map/pool/pallas_call | solution.py:232
  4.7 36.4 %all_to_all.20 = bf16[24,8,1024]{2,1,0:T(8,128)(2,1)S(1)} all-to-all(bf16[24,8,1024]{2,1,0:T(8,128)(2,1)S(1)} %bitcast.15), channel_id=1, replica_groups=mesh['x'=4,'y'=8,'core'=2,'dp'=12] {'core','dp'}, dimensions={0} | all-to-all | bytes 786432 | tf_op jit(solution)/shard_map/pooled_exchange/all_to_all | solution.py:254
  41.2 0.1 owned.1
  41.2 19.0 %all_to_all.21 = bf16[8,8,2048]{2,1,0:T(8,128)(2,1)S(1)} all-to-all(bf16[8,8,2048]{2,1,0:T(8,128)(2,1)S(1)} %get-tuple-element.10), channel_id=1, replica_groups=mesh['x'=4,'y'=8,'core'=2,'dp'=12] {'y'}, dimensions={0} | all-to-all | bytes 524288 | tf_op jit(solution)/shard_map/embed_exchange/all_to_all | solution.py:265
  60.2 0.1 broadcast_in_dim.3
  60.3 18.0 %all_to_all.22 = bf16[4,64,2048]{2,1,0:T(8,128)(2,1)S(1)} all-to-all(bf16[4,64,2048]{2,1,0:T(8,128)(2,1)S(1)} %broadcast_in_dim.3), channel_id=1, replica_groups=mesh['x'=4,'y'=8,'core'=2,'dp'=12] {'x'}, dimensions={0} | all-to-all | bytes 2097152 | tf_op jit(solution)/shard_map/embed_exchange/all_to_all | solution.py:267
  78.4 0.0 copy-start
  78.4 0.0 copy-start.1
  78.4 0.0 copy-start.2
  78.4 0.0 copy-start.3
  78.4 0.5 gram.1
  78.8 3.8 %all-gather = f32[512,256]{1,0:T(8,128)S(1)} all-gather(f32[256,256]{1,0:T(8,128)S(1)} %gram.1), channel_id=2, replica_groups=mesh['x'=4,'y'=8,'core'=2,'dp'=12] {'core'}, dimensions={0}, use_global_device_ids=true | all-gather | bytes 786432 | tf_op jit(solution)/shard_map/gram/all_gather | solution.py:276
  82.6 0.8 contrast.1
  83.5 23.0 %all_to_all.23 = bf16[24,8,1024]{2,1,0:T(8,128)(2,1)S(1)} all-to-all(bf16[24,8,1024]{2,1,0:T(8,128)(2,1)S(1)} %bitcast.14), channel_id=1, replica_groups=mesh['x'=4,'y'=8,'core'=2,'dp'=12] {'core','dp'}, dimensions={0} | all-to-all | bytes 786432 | tf_op jit(solution)/shard_map/grad_exchange/all_to_all | solution.py:286
  106.5 0.0 copy-done
  106.5 0.0 copy-done.1
  106.5 0.0 copy-done.2
  106.5 0.0 copy-done.3
  106.5 4.0 %rows.1 = bf16[1,256,4096]{2,1,0:T(8,128)(2,1)} custom-call(bf16[2,96,1024]{2,1,0:T(8,128)(2,1)S(1)} %bitcast.13, bf16[1,256,4096]{2,1,0:T(8,128)(2,1)S(1)} %copy-done, s32[1,1,256]{2,1,0:T(1,128)S(1)} %copy-done.2, s32[1,4]{1,0:T(1,128)S(1)} %copy-done.3, f32[1,4096]{1,0:T(1,128)S(1)} %bitcast.17, f32[256,128]{1,0:T(8,128)S(1)} %get-tuple-element.15.upright_ref), custom_call_target="tpu_custom_call" | custom-call | tf_op jit(solution)/shard_map/rows/pallas_call | solution.py:289
Async XLA Ops:
  78.4 28.1 %copy-start = (bf16[1,256,4096]{2,1,0:T(8,128)(2,1)S(1)}, bf16[1,256,4096]{2,1,0:T(8,128)(2,1)}, u32[]{:S(2)}) copy-start(bf16[1,256,4096]{2,1,0:T(8,128)(2,1)} %hidden_ref.1) | copy-start | bytes 6291460
  78.4 28.1 %copy-start.1 = (f32[4096]{0:T(1024)S(1)}, f32[4096]{0:T(1024)}, u32[]{:S(2)}) copy-start(f32[4096]{0:T(1024)} %param.9) | copy-start | bytes 49156
  78.4 28.1 %copy-start.2 = (s32[1,1,256]{2,1,0:T(1,128)S(1)}, s32[1,1,256]{2,1,0:T(1,128)}, u32[]{:S(2)}) copy-start(s32[1,1,256]{2,1,0:T(1,128)} %segment_ref.1) | copy-start | bytes 3076
  78.4 28.1 %copy-start.3 = (s32[1,4]{1,0:T(1,128)S(1)}, s32[1,4]{1,0:T(1,128)}, u32[]{:S(2)}) copy-start(s32[1,4]{1,0:T(1,128)} %assign_ref.1) | copy-start | bytes 52

commit v4 on v3

v4 whole, which is shorter than its diff:
```python
import functools

import jax
import jax.numpy as jnp
from jax import lax
from jax.experimental import pallas as pl
from jax.experimental.pallas import tpu as pltpu
from jax.sharding import Mesh
from jax.sharding import PartitionSpec as P

inv_tau = 20.0
loss_scale = 1024.0
norm_eps = 1e-06

F32 = jnp.float32
BF16 = jnp.bfloat16
ROWS = 256
D = 4096
HALF = D // 2
QUARTER = D // 4
PAS = 4
CHUNK = 1024
META = 128
N_ZH = 3
N_ZL = 4
N_X = 4
N_Y = 8
BATCH = 256

VMEM = pl.BlockSpec(memory_space=pltpu.VMEM)
HBM = pl.BlockSpec(memory_space=pltpu.HBM)
PARAMS = pltpu.CompilerParams(vmem_limit_bytes=40 * 1024 * 1024)


def iota(shape, dim):
    return lax.broadcasted_iota(jnp.int32, shape, dim)


def split3(values):
    high = values.astype(BF16).astype(F32)
    rest = values - high
    middle = rest.astype(BF16).astype(F32)
    low = rest - middle
    return jnp.concatenate([high, middle, low], axis=0).astype(BF16)


def sum3(values):
    return values[0:8] + values[8:16] + values[16:24]


def pool_kernel(
    hidden_hbm, segment_hbm, assign_hbm, gain_hbm, positive_hbm,
    send_ref, upright_ref, partner_ref,
    hidden, segment_at, assign_at, gain, positive, chunk_sem, small_sem,
):
    chunks = [pl.ds(at * CHUNK, CHUNK) for at in range(D // CHUNK)]
    copies = [
        pltpu.make_async_copy(hidden_hbm.at[0, :, part], hidden.at[:, part], chunk_sem.at[at])
        for at, part in enumerate(chunks)
    ]
    small = [
        pltpu.make_async_copy(source, target, small_sem.at[at])
        for at, (source, target) in enumerate(
            [(segment_hbm, segment_at), (assign_hbm, assign_at), (positive_hbm, positive), (gain_hbm, gain)]
        )
    ]
    copies[0].start()
    for copy in small:
        copy.start()
    for copy in copies[1:]:
        copy.start()

    for copy in small:
        copy.wait()
    segment = jnp.broadcast_to(segment_at[0], (8, ROWS))
    onehot = jnp.where(segment == iota((8, ROWS), 0), 1.0, 0.0)
    counts = jnp.maximum(jnp.sum(onehot, axis=1, keepdims=True), 1.0)
    row = iota((8, META), 0)
    owner = jnp.zeros((8, META), jnp.int32)
    for k in range(PAS):
        owner = jnp.where(lax.rem(row, PAS) == k, assign_at[0:1, k : k + 1], owner)
    place = lax.axis_index("core") * 32 + lax.axis_index("zl") * 8 + row
    meta = jnp.where(iota((8, META), 1) == place, owner, 0).astype(F32).astype(BF16)
    for h in range(2):
        for peer in range(N_ZL):
            send_ref[h, peer, :, QUARTER:] = meta
    lane = iota((64, BATCH), 1)
    spread = jnp.where(lax.div(lane, PAS) == iota((64, BATCH), 0), 1.0, 0.0).astype(BF16)
    partner = jnp.concatenate([positive[...].astype(F32), jnp.zeros((PAS, 64), F32)], axis=0)
    partner = jnp.dot(partner.astype(BF16), spread, preferred_element_type=F32)
    partner = jnp.where(lax.rem(iota((8, BATCH), 1), PAS) == iota((8, BATCH), 0), partner, 0.0)
    partner_ref[...] = jnp.sum(partner, axis=0, keepdims=True).astype(jnp.int32)

    products = jnp.zeros((ROWS, ROWS), F32)
    for at, part in enumerate(chunks):
        copies[at].wait()
        values = hidden[:, part]
        products = products + lax.dot_general(
            values, values, (((1,), (1,)), ((), ())), preferred_element_type=F32
        )
    products = jnp.where(iota((ROWS, ROWS), 0) == iota((ROWS, ROWS), 1), products, 0.0)
    squares = jnp.sum(products, axis=0, keepdims=True)
    inverse = jnp.broadcast_to(lax.rsqrt(squares * (1.0 / D) + norm_eps), (8, ROWS))
    weights = split3(onehot * inverse)
    for h in range(2):
        columns = pl.ds(h * HALF, HALF)
        pooled = sum3(jnp.dot(weights, hidden[:, columns], preferred_element_type=F32))
        pooled = (pooled * gain[:, columns] / counts)[0:PAS]
        pooled = jnp.concatenate([pooled[:, 0:QUARTER], pooled[:, QUARTER:]], axis=0).astype(BF16)
        for peer in range(N_ZL):
            send_ref[h, peer, :, 0:QUARTER] = pooled
    upright_ref[...] = jnp.concatenate(
        [onehot, onehot, onehot, inverse, jnp.zeros((96, ROWS), F32)], axis=0
    ).T


def relay_kernel(pooled_ref, send_ref, back_ref):
    relay = lax.axis_index("zl")
    owners = jnp.sum(pooled_ref[:, QUARTER:].astype(F32), axis=0, keepdims=True)
    row = iota((128, META), 0)
    lane = iota((128, META), 1)
    slot = (lax.div(row, 8) * N_ZL + relay) * PAS + lax.rem(row, PAS)
    hit = (owners == slot.astype(F32)) & (lax.div(lane, 32) == lax.div(lax.rem(row, 8), PAS))
    hit = hit & (row < N_ZH * 8) & (lane < 64)
    select = jnp.where(hit, 1.0, 0.0)
    back_ref[...] = select.T
    pooled = pooled_ref[:, 0:QUARTER]
    for q in range(2):
        part = jnp.where(lax.rem(lax.div(lane, PAS), 2) == q, select, 0.0)[0 : N_ZH * 8, 0:64]
        kept = jnp.dot(part.astype(BF16), pooled, preferred_element_type=F32)
        for peer in range(N_ZH):
            send_ref[peer, :, q * QUARTER : (q + 1) * QUARTER] = kept[
                peer * 8 : (peer + 1) * 8
            ].astype(BF16)


def owned_kernel(pooled_ref, send_ref, embed_ref):
    own = pooled_ref[0].astype(F32)
    for peer in range(1, N_ZH):
        own = own + pooled_ref[peer].astype(F32)
    embed_ref[...] = own
    own = own.astype(BF16)
    for peer in range(N_Y):
        send_ref[peer] = own


def gram_kernel(embed_ref, gram_ref):
    embeds = embed_ref[...]
    gram_ref[...] = lax.dot_general(
        embeds, embeds, (((1,), (1,)), ((), ())), preferred_element_type=F32
    )


def contrast_kernel(gram_ref, batch_ref, embed_ref, partner_ref, loss_ref, send_ref):
    core = lax.axis_index("core")
    first = (lax.axis_index("x") * 8 + lax.axis_index("y")) * 8
    shift = inv_tau
    row = iota((8, BATCH), 0)
    lane = iota((8, BATCH), 1)
    mine = first + row
    partner = partner_ref[...]
    own_partner = jnp.sum(jnp.where(lane == mine, partner, 0), axis=1, keepdims=True)

    gram = gram_ref[0] + gram_ref[1]
    everyone = iota((BATCH, BATCH), 0) == iota((BATCH, BATCH), 1)
    diagonal = jnp.where(everyone, gram, 0.0)
    across = lax.rsqrt(jnp.sum(diagonal, axis=0, keepdims=True) + norm_eps)
    down = lax.rsqrt(jnp.sum(diagonal, axis=1, keepdims=True) + norm_eps)
    logits = jnp.where(everyone, -1e30, gram * down * across * inv_tau)
    lse_all = shift + jnp.log(jnp.sum(jnp.exp(logits - shift), axis=0, keepdims=True))
    at = pl.ds(pl.multiple_of(first, 8), 8)
    own = gram_ref[0, at, :] + gram_ref[1, at, :]
    scale = lax.rsqrt(
        jnp.sum(jnp.where(lane == mine, own, 0.0), axis=1, keepdims=True) + norm_eps
    )
    cosine = own * scale * across
    own = jnp.where(lane == mine, -1e30, cosine * inv_tau)
    lse = shift + jnp.log(jnp.sum(jnp.exp(own - shift), axis=1, keepdims=True))
    hits = lane == own_partner
    loss = lse - jnp.sum(jnp.where(hits, own, 0.0), axis=1, keepdims=True)
    as_query = loss_scale * (jnp.exp(own - lse) - jnp.where(hits, 1.0, 0.0))
    as_key = loss_scale * (jnp.exp(own - lse_all) - jnp.where(partner == mine, 1.0, 0.0))
    weights = as_query.astype(BF16).astype(F32) + as_key.astype(BF16).astype(F32)
    inner = inv_tau * jnp.sum(weights * cosine, axis=1, keepdims=True)
    pair = jnp.concatenate([as_query, as_key], axis=0).astype(BF16)
    width = 512
    for start in range(0, HALF, width):
        columns = pl.ds(start, width)
        units = (batch_ref[:, columns].astype(F32) * down).astype(BF16)
        grad = jnp.dot(pair, units, preferred_element_type=F32)
        grad = (grad[0:8] + grad[8:16]) * inv_tau - embed_ref[:, columns] * (scale * inner)
        grad = (grad * scale).astype(BF16)
        for peer in range(N_ZH):
            send_ref[peer, :, columns] = grad
    place = (iota((8, 128), 1) + core * PAS) == iota((8, 128), 0)
    loss = jnp.sum(jnp.where(place, loss, 0.0), axis=0, keepdims=True)
    loss_ref[...] = loss[:, 0:PAS]


def back_kernel(grad_ref, back_ref, send_ref):
    back = back_ref[...]
    row = iota((128, META), 0)
    total = jnp.zeros((64, QUARTER), F32)
    for q in range(2):
        part = jnp.where(lax.rem(lax.div(row, PAS), 2) == q, back, 0.0)[0:64, 0 : N_ZH * 8]
        total = total + jnp.dot(
            part.astype(BF16),
            grad_ref[:, q * QUARTER : (q + 1) * QUARTER],
            preferred_element_type=F32,
        )
    total = total.astype(BF16)
    for c in range(2):
        for peer in range(N_ZL):
            at = (c * N_ZL + peer) * 8
            send_ref[c, peer] = total[at : at + 8]


def rows_kernel(
    grad_ref, hidden_ref, segment_ref, gain_ref, upright_ref, out_hbm,
    scaled, coef, out, sems, gained_ref,
):
    segment = jnp.broadcast_to(segment_ref[0], (8, ROWS))
    onehot = jnp.where(segment == iota((8, ROWS), 0), 1.0, 0.0)
    counts = jnp.maximum(jnp.sum(onehot, axis=1, keepdims=True), 1.0)
    for h in range(2):
        part = grad_ref[h, 0].astype(F32)
        for peer in range(1, N_ZL):
            part = part + grad_ref[h, peer].astype(F32)
        for q in range(2):
            columns = pl.ds((h * 2 + q) * QUARTER, QUARTER)
            scaled[:, columns] = split3(gain_ref[:, columns] * (part / counts))
            part = jnp.concatenate([part[PAS:], part[0:PAS]], axis=0)
    upright = upright_ref[...]
    spread = upright[:, 0:24]
    inverse = upright[:, 24:25]
    low = spread.astype(BF16)
    width = 512
    total = jnp.zeros((ROWS, 128), F32)
    for at in range(0, D, width):
        columns = pl.ds(at, width)
        part = jnp.dot(low, scaled[:, columns], preferred_element_type=F32)
        gained_ref[:, columns] = part
        part = part * hidden_ref[0, :, columns].astype(F32)
        for piece in range(0, width, 128):
            total = total + part[:, piece : piece + 128]
    dot = jnp.sum(total, axis=1, keepdims=True) * (1.0 / D)
    coef[:, 0:128] = jnp.broadcast_to(inverse, (ROWS, 128))
    coef[:, 128:256] = jnp.broadcast_to(inverse * inverse * inverse * dot, (ROWS, 128))
    copies = []
    for at in range(0, D, width):
        columns = pl.ds(at, width)
        gained = gained_ref[:, columns]
        values = hidden_ref[0, :, columns].astype(F32)
        out[:, columns] = (coef[:, 0:1] * gained - values * coef[:, 128:129]).astype(BF16)
        copy = pltpu.make_async_copy(
            out.at[:, columns], out_hbm.at[0, :, columns], sems.at[at // width]
        )
        copy.start()
        copies.append(copy)
    for copy in copies:
        copy.wait()


def local(hidden, segment_ids, assign, positive, gain):
    shape = jax.ShapeDtypeStruct
    gain = gain.reshape(1, D)
    with jax.named_scope("pool"):
        send, upright, partner = pl.pallas_call(
            pool_kernel,
            out_shape=(
                shape((2, N_ZL, 8, QUARTER + META), BF16),
                shape((ROWS, 128), F32),
                shape((1, BATCH), jnp.int32),
            ),
            in_specs=[HBM] * 5,
            out_specs=(VMEM, VMEM, VMEM),
            scratch_shapes=[
                pltpu.VMEM((ROWS, D), BF16),
                pltpu.VMEM((1, 1, ROWS), jnp.int32),
                pltpu.VMEM((1, PAS), jnp.int32),
                pltpu.VMEM((1, D), F32),
                pltpu.VMEM((PAS, 64), jnp.int32),
                pltpu.SemaphoreType.DMA((D // CHUNK,)),
                pltpu.SemaphoreType.DMA((4,)),
            ],
            compiler_params=PARAMS,
        )(*[pltpu.with_memory_space_constraint(v, pltpu.HBM) for v in (hidden, segment_ids, assign, gain, positive.T)])
    with jax.named_scope("pooled_to_relay"):
        pooled = lax.all_to_all(send.reshape(2 * N_ZL, 8, -1), ("core", "zl"), 0, 0)
        pooled = pooled.reshape(2 * N_ZL * 8, -1)
    with jax.named_scope("relay"):
        send, back = pl.pallas_call(
            relay_kernel,
            out_shape=(shape((N_ZH, 8, HALF), BF16), shape((128, META), F32)),
            in_specs=[VMEM],
            out_specs=(VMEM, VMEM),
            compiler_params=PARAMS,
        )(pooled)
    with jax.named_scope("pooled_to_owner"):
        pooled = lax.all_to_all(send, "zh", 0, 0)
    with jax.named_scope("owned"):
        send, embed = pl.pallas_call(
            owned_kernel,
            out_shape=(shape((N_Y, 8, HALF), BF16), shape((8, HALF), F32)),
            in_specs=[VMEM],
            out_specs=(VMEM, VMEM),
            compiler_params=PARAMS,
        )(pooled)
    with jax.named_scope("embed_exchange"):
        batch = lax.all_to_all(send, "y", 0, 0).reshape(N_Y * 8, HALF)
        batch = jnp.broadcast_to(batch, (N_X, N_Y * 8, HALF))
        batch = lax.all_to_all(batch, "x", 0, 0).reshape(BATCH, HALF)
    with jax.named_scope("gram"):
        gram = pl.pallas_call(
            gram_kernel,
            out_shape=shape((BATCH, BATCH), F32),
            in_specs=[VMEM],
            out_specs=VMEM,
            compiler_params=PARAMS,
        )(batch)
        gram = lax.all_gather(gram, "core", axis=0)
    with jax.named_scope("contrast"):
        loss, send = pl.pallas_call(
            contrast_kernel,
            out_shape=(shape((1, PAS), F32), shape((N_ZH, 8, HALF), BF16)),
            in_specs=[VMEM] * 4,
            out_specs=(VMEM, VMEM),
            compiler_params=PARAMS,
        )(gram, batch, embed, partner)
    with jax.named_scope("grad_to_relay"):
        grads = lax.all_to_all(send, "zh", 0, 0).reshape(N_ZH * 8, HALF)
    with jax.named_scope("back"):
        send = pl.pallas_call(
            back_kernel,
            out_shape=shape((2, N_ZL, 8, QUARTER), BF16),
            in_specs=[VMEM, VMEM],
            out_specs=VMEM,
            compiler_params=PARAMS,
        )(grads, back)
    with jax.named_scope("grad_to_rows"):
        grads = lax.all_to_all(send.reshape(2 * N_ZL, 8, QUARTER), ("core", "zl"), 0, 0)
        grads = grads.reshape(2, N_ZL, 8, QUARTER)
    with jax.named_scope("rows"):
        grad_rows = pl.pallas_call(
            rows_kernel,
            out_shape=shape((1, ROWS, D), BF16),
            in_specs=[VMEM] * 5,
            out_specs=HBM,
            scratch_shapes=[
                pltpu.VMEM((24, D), BF16),
                pltpu.VMEM((ROWS, 256), F32),
                pltpu.VMEM((ROWS, D), BF16),
                pltpu.SemaphoreType.DMA((8,)),
                pltpu.VMEM((ROWS, D), F32),
            ],
            compiler_params=PARAMS,
        )(grads, hidden, segment_ids, gain, upright)
    return loss, grad_rows


def solution(mesh):
    fine = Mesh(
        mesh.devices.reshape(N_X, N_Y, 2, N_ZH, N_ZL), ("x", "y", "core", "zh", "zl")
    )
    group, dp = ("x", "y", "core"), ("zh", "zl")
    placed = (P(group, dp, None), P(group, dp, None), P(group, dp), P(None, dp), P())
    return jax.shard_map(
        local,
        mesh=fine,
        in_specs=placed,
        out_specs=(P(group, dp), P(group, dp, None)),
        check_vma=False,
    )
```

time: 111 us -> 104 us (0.937)
  blocking collectives: 100 us -> 94.9 us
  Pallas kernels: 9.5 us -> 8.18 us
    all_to_all x2 -> x4, blocking collectives: 59.5 us -> 56.3 us  [the longest x1 19.7 us: local(): pooled = lax.all_to_all(send.reshape(2 * N_ZL, 8, -1), ('core', 'zl'), 0, 0)]
    all_to_all x1, blocking collectives: 19 us -> 16.8 us  [local(): batch = lax.all_to_all(send, 'y', 0, 0).reshape(N_Y * 8, HALF)]
    all_gather x1, blocking collectives: 3.78 us -> 5.92 us  [local(): gram = lax.all_gather(gram, 'core', axis=0)]
    all_to_all x1, blocking collectives: 18 us -> 15.9 us  [local(): batch = lax.all_to_all(batch, 'x', 0, 0).reshape(BATCH, HALF)]
    pallas_call x2 -> x4, Pallas kernels: 4.93 us -> 4.68 us  [the longest x1 3.41 us: local(): pl.pallas_call(pool_kernel, out_shape=(shape((2, N_ZL, 8, QUARTER + META)...]
where the time goes in v4:
time: 104 us
  blocking collectives  94.9 us (91%)
  Pallas kernels  8.18 us (8%)
    all_to_all x1, blocking collectives, local(): pooled = lax.all_to_all(send.reshape(2 * N_ZL, 8, -1), ('core', 'zl'), 0, 0)  19.7 us
    all_to_all x1, blocking collectives, local(): batch = lax.all_to_all(send, 'y', 0, 0).reshape(N_Y * 8, HALF)  16.8 us
    all_to_all x1, blocking collectives, local(): batch = lax.all_to_all(batch, 'x', 0, 0).reshape(BATCH, HALF)  15.9 us
    all_to_all x1, blocking collectives, local(): pooled = lax.all_to_all(send, 'zh', 0, 0)  15.4 us
    all_to_all x1, blocking collectives, local(): lax.all_to_all(send.reshape(2 * N_ZL, 8, QUARTER), ('core', 'zl'), 0, 0)  10.7 us
    all_to_all x1, blocking collectives, local(): grads = lax.all_to_all(send, 'zh', 0, 0).reshape(N_ZH * 8, HALF)  10.4 us
    all_gather x1, blocking collectives, local(): gram = lax.all_gather(gram, 'core', axis=0)  5.92 us
    pallas_call x1, Pallas kernels, local(): pl.pallas_call(pool_kernel, out_shape=(shape((2, N_ZL, 8, QUARTER + META)...  3.41 us

profile of v4, /device:TPU:1, one launch (start us, length us, event | category | flops | bytes accessed | tf_op | source)
XLA Modules:
  0.0 103.9 jit_solution(2928145230971469964)
XLA Ops:
  0.6 3.4 %pool.1 = (bf16[2,4,8,1152]{3,2,1,0:T(8,128)(2,1)S(1)}, f32[256,128]{1,0:T(8,128)S(1)}, s32[1,256]{1,0:T(1,128)S(1)}) custom-call(bf16[1,256,4096]{2,1,0:T(8,128)(2,1)} %hidden_ref.1, s32[1,1,256]{2,1,0:T(1,128)} %segment_ref.1, s32[1,4]{1,0:T(1,128)} %assign_hbm.1, f32[1,4096]{1,0:T(1,128)} %bitcast.18, s32[4,64]{1,0:T(4,128)} %bitcast.21), custom_call_target="tpu_custom_call" | custom-call | tf_op jit(solution)/shard_map/pool/pallas_call | solution.py:268
  4.1 19.7 %all_to_all.30 = bf16[8,8,1152]{2,1,0:T(8,128)(2,1)S(1)} all-to-all(bf16[8,8,1152]{2,1,0:T(8,128)(2,1)S(1)} %bitcast.17), channel_id=1, replica_groups=mesh['x'=4,'y'=8,'core'=2,'zh'=3,'zl'=4] {'core','zl'}, dimensions={0} | all-to-all | bytes 294912 | tf_op jit(solution)/shard_map/pooled_to_relay/all_to_all | solution.py:289
  23.8 0.2 relay.1
  23.9 15.4 %all_to_all.31.pooled_ref = bf16[3,8,2048]{2,1,0:T(8,128)(2,1)S(1)} all-to-all(bf16[3,8,2048]{2,1,0:T(8,128)(2,1)S(1)} %get-tuple-element.12), channel_id=1, replica_groups=mesh['x'=4,'y'=8,'core'=2,'zh'=3,'zl'=4] {'zh'}, dimensions={0} | all-to-all | bytes 196608 | tf_op jit(solution)/shard_map/pooled_to_owner/all_to_all | solution.py:300
  39.4 16.8 %all_to_all.32 = bf16[8,8,2048]{2,1,0:T(8,128)(2,1)S(1)} all-to-all(bf16[8,8,2048]{2,1,0:T(8,128)(2,1)S(1)} %get-tuple-element.13), channel_id=1, replica_groups=mesh['x'=4,'y'=8,'core'=2,'zh'=3,'zl'=4] {'y'}, dimensions={0} | all-to-all | bytes 524288 | tf_op jit(solution)/shard_map/embed_exchange/all_to_all | solution.py:310
  56.2 0.1 broadcast_in_dim.3
  56.3 15.9 %all_to_all.33 = bf16[4,64,2048]{2,1,0:T(8,128)(2,1)S(1)} all-to-all(bf16[4,64,2048]{2,1,0:T(8,128)(2,1)S(1)} %broadcast_in_dim.3), channel_id=1, replica_groups=mesh['x'=4,'y'=8,'core'=2,'zh'=3,'zl'=4] {'x'}, dimensions={0} | all-to-all | bytes 2097152 | tf_op jit(solution)/shard_map/embed_exchange/all_to_all | solution.py:312
  72.2 0.0 copy-start
  72.2 0.0 copy-start.1
  72.2 0.0 copy-start.2
  72.2 0.5 gram.1
  72.7 5.9 %all-gather = f32[512,256]{1,0:T(8,128)S(1)} all-gather(f32[256,256]{1,0:T(8,128)S(1)} %gram.1), channel_id=2, replica_groups=mesh['x'=4,'y'=8,'core'=2,'zh'=3,'zl'=4] {'core'}, dimensions={0}, use_global_device_ids=true | all-gather | bytes 786432 | tf_op jit(solution)/shard_map/gram/all_gather | solution.py:321
  78.6 0.9 contrast.1
  79.5 10.4 %all_to_all.34 = bf16[3,8,2048]{2,1,0:T(8,128)(2,1)S(1)} all-to-all(bf16[3,8,2048]{2,1,0:T(8,128)(2,1)S(1)} %get-tuple-element.17), channel_id=1, replica_groups=mesh['x'=4,'y'=8,'core'=2,'zh'=3,'zl'=4] {'zh'}, dimensions={0} | all-to-all | bytes 196608 | tf_op jit(solution)/shard_map/grad_to_relay/all_to_all | solution.py:331
  89.9 0.2 back.1
  90.1 10.7 %all_to_all.35 = bf16[8,8,1024]{2,1,0:T(8,128)(2,1)S(1)} all-to-all(bf16[8,8,1024]{2,1,0:T(8,128)(2,1)S(1)} %bitcast.15), channel_id=1, replica_groups=mesh['x'=4,'y'=8,'core'=2,'zh'=3,'zl'=4] {'core','zl'}, dimensions={0} | all-to-all | bytes 262144 | tf_op jit(solution)/shard_map/grad_to_rows/all_to_all | solution.py:341
  100.9 0.0 copy-done
  100.9 0.0 copy-done.1
  100.9 0.0 copy-done.2
  100.9 3.0 %rows.1 = bf16[1,256,4096]{2,1,0:T(8,128)(2,1)} custom-call(bf16[2,4,8,1024]{3,2,1,0:T(8,128)(2,1)S(1)} %bitcast.14, bf16[1,256,4096]{2,1,0:T(8,128)(2,1)S(1)} %copy-done, s32[1,1,256]{2,1,0:T(1,128)S(1)} %copy-done.2, f32[1,4096]{1,0:T(1,128)S(1)} %bitcast.19, f32[256,128]{1,0:T(8,128)S(1)} %get-tuple-element.19.upright_ref), custom_call_target="tpu_custom_call" | custom-call | tf_op jit(solution)/shard_map/rows/pallas_call | solution.py:344
  (1 shorter events, 0.0 us)
Async XLA Ops:
  72.2 28.7 %copy-start = (bf16[1,256,4096]{2,1,0:T(8,128)(2,1)S(1)}, bf16[1,256,4096]{2,1,0:T(8,128)(2,1)}, u32[]{:S(2)}) copy-start(bf16[1,256,4096]{2,1,0:T(8,128)(2,1)} %hidden_ref.1) | copy-start | bytes 6291460
  72.2 28.7 %copy-start.1 = (f32[4096]{0:T(1024)S(1)}, f32[4096]{0:T(1024)}, u32[]{:S(2)}) copy-start(f32[4096]{0:T(1024)} %param.9) | copy-start | bytes 49156
  72.2 28.7 %copy-start.2 = (s32[1,1,256]{2,1,0:T(1,128)S(1)}, s32[1,1,256]{2,1,0:T(1,128)}, u32[]{:S(2)}) copy-start(s32[1,1,256]{2,1,0:T(1,128)} %segment_ref.1) | copy-start | bytes 3076

commit v5 on v4

--- a/solution.py
+++ b/solution.py
@@ -20,6 +20,7 @@
 QUARTER = D // 4
 PAS = 4
 CHUNK = 1024
+BLOCK = 64
 META = 128
 N_ZH = 3
 N_ZL = 4
@@ -91,15 +92,13 @@
     partner = jnp.where(lax.rem(iota((8, BATCH), 1), PAS) == iota((8, BATCH), 0), partner, 0.0)
     partner_ref[...] = jnp.sum(partner, axis=0, keepdims=True).astype(jnp.int32)
 
-    products = jnp.zeros((ROWS, ROWS), F32)
+    total = jnp.zeros((ROWS, 128), F32)
     for at, part in enumerate(chunks):
         copies[at].wait()
-        values = hidden[:, part]
-        products = products + lax.dot_general(
-            values, values, (((1,), (1,)), ((), ())), preferred_element_type=F32
-        )
-    products = jnp.where(iota((ROWS, ROWS), 0) == iota((ROWS, ROWS), 1), products, 0.0)
-    squares = jnp.sum(products, axis=0, keepdims=True)
+        for piece in range(0, CHUNK, 128):
+            values = hidden[:, at * CHUNK + piece : at * CHUNK + piece + 128].astype(F32)
+            total = total + values * values
+    squares = jnp.sum(total.T, axis=0, keepdims=True)
     inverse = jnp.broadcast_to(lax.rsqrt(squares * (1.0 / D) + norm_eps), (8, ROWS))
     weights = split3(onehot * inverse)
     for h in range(2):
@@ -217,7 +216,7 @@
 
 def rows_kernel(
     grad_ref, hidden_ref, segment_ref, gain_ref, upright_ref, out_hbm,
-    scaled, coef, out, sems, gained_ref,
+    scaled, gained, out, sems,
 ):
     segment = jnp.broadcast_to(segment_ref[0], (8, ROWS))
     onehot = jnp.where(segment == iota((8, ROWS), 0), 1.0, 0.0)
@@ -230,31 +229,27 @@
             columns = pl.ds((h * 2 + q) * QUARTER, QUARTER)
             scaled[:, columns] = split3(gain_ref[:, columns] * (part / counts))
             part = jnp.concatenate([part[PAS:], part[0:PAS]], axis=0)
-    upright = upright_ref[...]
-    spread = upright[:, 0:24]
-    inverse = upright[:, 24:25]
-    low = spread.astype(BF16)
-    width = 512
-    total = jnp.zeros((ROWS, 128), F32)
-    for at in range(0, D, width):
-        columns = pl.ds(at, width)
-        part = jnp.dot(low, scaled[:, columns], preferred_element_type=F32)
-        gained_ref[:, columns] = part
-        part = part * hidden_ref[0, :, columns].astype(F32)
-        for piece in range(0, width, 128):
-            total = total + part[:, piece : piece + 128]
-    dot = jnp.sum(total, axis=1, keepdims=True) * (1.0 / D)
-    coef[:, 0:128] = jnp.broadcast_to(inverse, (ROWS, 128))
-    coef[:, 128:256] = jnp.broadcast_to(inverse * inverse * inverse * dot, (ROWS, 128))
+    width = 1024
     copies = []
-    for at in range(0, D, width):
-        columns = pl.ds(at, width)
-        gained = gained_ref[:, columns]
-        values = hidden_ref[0, :, columns].astype(F32)
-        out[:, columns] = (coef[:, 0:1] * gained - values * coef[:, 128:129]).astype(BF16)
-        copy = pltpu.make_async_copy(
-            out.at[:, columns], out_hbm.at[0, :, columns], sems.at[at // width]
-        )
+    for start in range(0, ROWS, BLOCK):
+        rows = pl.ds(start, BLOCK)
+        spread = upright_ref[rows, 0:24].astype(BF16)
+        inverse = upright_ref[rows, 24:25]
+        total = jnp.zeros((BLOCK, 128), F32)
+        for at in range(0, D, width):
+            columns = pl.ds(at, width)
+            part = jnp.dot(spread, scaled[:, columns], preferred_element_type=F32)
+            gained[:, columns] = part
+            part = part * hidden_ref[0, rows, columns].astype(F32)
+            for piece in range(0, width, 128):
+                total = total + part[:, piece : piece + 128]
+        dot = jnp.sum(total, axis=1, keepdims=True) * (1.0 / D)
+        cubed = inverse * inverse * inverse * dot
+        for at in range(0, D, width):
+            columns = pl.ds(at, width)
+            values = hidden_ref[0, rows, columns].astype(F32)
+            out[rows, columns] = (inverse * gained[:, columns] - values * cubed).astype(BF16)
+        copy = pltpu.make_async_copy(out.at[rows], out_hbm.at[0, rows], sems.at[start // BLOCK])
         copy.start()
         copies.append(copy)
     for copy in copies:
@@ -348,10 +343,9 @@
             out_specs=HBM,
             scratch_shapes=[
                 pltpu.VMEM((24, D), BF16),
-                pltpu.VMEM((ROWS, 256), F32),
+                pltpu.VMEM((BLOCK, D), F32),
                 pltpu.VMEM((ROWS, D), BF16),
-                pltpu.SemaphoreType.DMA((8,)),
-                pltpu.VMEM((ROWS, D), F32),
+                pltpu.SemaphoreType.DMA((ROWS // BLOCK,)),
             ],
             compiler_params=PARAMS,
         )(grads, hidden, segment_ids, gain, upright)

time: 104 us -> 103 us (level)
  Pallas kernels: 8.18 us -> 6.77 us
where the time goes in v5:
time: 103 us; the launch traced here: 102 us
  blocking collectives  94.9 us (92%)
  Pallas kernels  6.77 us (7%)
    all_to_all x1, blocking collectives, local(): pooled = lax.all_to_all(send.reshape(2 * N_ZL, 8, -1), ('core', 'zl'), 0, 0)  19.7 us
    all_to_all x1, blocking collectives, local(): batch = lax.all_to_all(send, 'y', 0, 0).reshape(N_Y * 8, HALF)  16.8 us
    all_to_all x1, blocking collectives, local(): batch = lax.all_to_all(batch, 'x', 0, 0).reshape(BATCH, HALF)  15.9 us
    all_to_all x1, blocking collectives, local(): pooled = lax.all_to_all(send, 'zh', 0, 0)  15.4 us
    all_to_all x1, blocking collectives, local(): lax.all_to_all(send.reshape(2 * N_ZL, 8, QUARTER), ('core', 'zl'), 0, 0)  10.7 us
    all_to_all x1, blocking collectives, local(): grads = lax.all_to_all(send, 'zh', 0, 0).reshape(N_ZH * 8, HALF)  10.4 us
    all_gather x1, blocking collectives, local(): gram = lax.all_gather(gram, 'core', axis=0)  5.92 us
    pallas_call x1, Pallas kernels, local(): pl.pallas_call(pool_kernel, out_shape=(shape((2, N_ZL, 8, QUARTER + META)...  2.61 us

profile of v5, /device:TPU:1, one launch (start us, length us, event | category | flops | bytes accessed | tf_op | source)
XLA Modules:
  0.0 102.5 jit_solution(11482237243650548927)
XLA Ops:
  0.6 2.6 %pool.1 = (bf16[2,4,8,1152]{3,2,1,0:T(8,128)(2,1)S(1)}, f32[256,128]{1,0:T(8,128)S(1)}, s32[1,256]{1,0:T(1,128)S(1)}) custom-call(bf16[1,256,4096]{2,1,0:T(8,128)(2,1)} %hidden_ref.1, s32[1,1,256]{2,1,0:T(1,128)} %segment_ref.1, s32[1,4]{1,0:T(1,128)} %assign_hbm.1, f32[1,4096]{1,0:T(1,128)} %bitcast.18, s32[4,64]{1,0:T(4,128)} %bitcast.21), custom_call_target="tpu_custom_call" | custom-call | tf_op jit(solution)/shard_map/pool/pallas_call | solution.py:263
  3.2 19.7 %all_to_all.30 = bf16[8,8,1152]{2,1,0:T(8,128)(2,1)S(1)} all-to-all(bf16[8,8,1152]{2,1,0:T(8,128)(2,1)S(1)} %bitcast.17), channel_id=1, replica_groups=mesh['x'=4,'y'=8,'core'=2,'zh'=3,'zl'=4] {'core','zl'}, dimensions={0} | all-to-all | bytes 294912 | tf_op jit(solution)/shard_map/pooled_to_relay/all_to_all | solution.py:284
  22.9 0.2 relay.1
  23.1 15.4 %all_to_all.31.pooled_ref = bf16[3,8,2048]{2,1,0:T(8,128)(2,1)S(1)} all-to-all(bf16[3,8,2048]{2,1,0:T(8,128)(2,1)S(1)} %get-tuple-element.12), channel_id=1, replica_groups=mesh['x'=4,'y'=8,'core'=2,'zh'=3,'zl'=4] {'zh'}, dimensions={0} | all-to-all | bytes 196608 | tf_op jit(solution)/shard_map/pooled_to_owner/all_to_all | solution.py:295
  38.6 16.8 %all_to_all.32 = bf16[8,8,2048]{2,1,0:T(8,128)(2,1)S(1)} all-to-all(bf16[8,8,2048]{2,1,0:T(8,128)(2,1)S(1)} %get-tuple-element.13), channel_id=1, replica_groups=mesh['x'=4,'y'=8,'core'=2,'zh'=3,'zl'=4] {'y'}, dimensions={0} | all-to-all | bytes 524288 | tf_op jit(solution)/shard_map/embed_exchange/all_to_all | solution.py:305
  55.4 0.1 broadcast_in_dim.3
  55.5 15.9 %all_to_all.33 = bf16[4,64,2048]{2,1,0:T(8,128)(2,1)S(1)} all-to-all(bf16[4,64,2048]{2,1,0:T(8,128)(2,1)S(1)} %broadcast_in_dim.3), channel_id=1, replica_groups=mesh['x'=4,'y'=8,'core'=2,'zh'=3,'zl'=4] {'x'}, dimensions={0} | all-to-all | bytes 2097152 | tf_op jit(solution)/shard_map/embed_exchange/all_to_all | solution.py:307
  71.4 0.0 copy-start
  71.4 0.0 copy-start.1
  71.4 0.0 copy-start.2
  71.4 0.5 gram.1
  71.9 5.9 %all-gather = f32[512,256]{1,0:T(8,128)S(1)} all-gather(f32[256,256]{1,0:T(8,128)S(1)} %gram.1), channel_id=2, replica_groups=mesh['x'=4,'y'=8,'core'=2,'zh'=3,'zl'=4] {'core'}, dimensions={0}, use_global_device_ids=true | all-gather | bytes 786432 | tf_op jit(solution)/shard_map/gram/all_gather | solution.py:316
  77.8 0.9 contrast.1
  78.7 10.4 %all_to_all.34 = bf16[3,8,2048]{2,1,0:T(8,128)(2,1)S(1)} all-to-all(bf16[3,8,2048]{2,1,0:T(8,128)(2,1)S(1)} %get-tuple-element.17), channel_id=1, replica_groups=mesh['x'=4,'y'=8,'core'=2,'zh'=3,'zl'=4] {'zh'}, dimensions={0} | all-to-all | bytes 196608 | tf_op jit(solution)/shard_map/grad_to_relay/all_to_all | solution.py:326
  89.1 0.2 back.1
  89.3 10.7 %all_to_all.35 = bf16[8,8,1024]{2,1,0:T(8,128)(2,1)S(1)} all-to-all(bf16[8,8,1024]{2,1,0:T(8,128)(2,1)S(1)} %bitcast.15), channel_id=1, replica_groups=mesh['x'=4,'y'=8,'core'=2,'zh'=3,'zl'=4] {'core','zl'}, dimensions={0} | all-to-all | bytes 262144 | tf_op jit(solution)/shard_map/grad_to_rows/all_to_all | solution.py:336
  100.1 0.0 copy-done
  100.1 0.0 copy-done.1
  100.1 0.0 copy-done.2
  100.1 2.4 %rows.1 = bf16[1,256,4096]{2,1,0:T(8,128)(2,1)} custom-call(bf16[2,4,8,1024]{3,2,1,0:T(8,128)(2,1)S(1)} %bitcast.14, bf16[1,256,4096]{2,1,0:T(8,128)(2,1)S(1)} %copy-done, s32[1,1,256]{2,1,0:T(1,128)S(1)} %copy-done.2, f32[1,4096]{1,0:T(1,128)S(1)} %bitcast.19, f32[256,128]{1,0:T(8,128)S(1)} %get-tuple-element.19.upright_ref), custom_call_target="tpu_custom_call" | custom-call | tf_op jit(solution)/shard_map/rows/pallas_call | solution.py:339
  (1 shorter events, 0.0 us)
Async XLA Ops:
  71.4 28.7 %copy-start = (bf16[1,256,4096]{2,1,0:T(8,128)(2,1)S(1)}, bf16[1,256,4096]{2,1,0:T(8,128)(2,1)}, u32[]{:S(2)}) copy-start(bf16[1,256,4096]{2,1,0:T(8,128)(2,1)} %hidden_ref.1) | copy-start | bytes 6291460
  71.4 28.7 %copy-start.1 = (f32[4096]{0:T(1024)S(1)}, f32[4096]{0:T(1024)}, u32[]{:S(2)}) copy-start(f32[4096]{0:T(1024)} %param.9) | copy-start | bytes 49156
  71.4 28.7 %copy-start.2 = (s32[1,1,256]{2,1,0:T(1,128)S(1)}, s32[1,1,256]{2,1,0:T(1,128)}, u32[]{:S(2)}) copy-start(s32[1,1,256]{2,1,0:T(1,128)} %segment_ref.1) | copy-start | bytes 3076

commit v6 on v5

--- a/solution.py
+++ b/solution.py
@@ -138,9 +138,7 @@
     for peer in range(1, N_ZH):
         own = own + pooled_ref[peer].astype(F32)
     embed_ref[...] = own
-    own = own.astype(BF16)
-    for peer in range(N_Y):
-        send_ref[peer] = own
+    send_ref[...] = own.astype(BF16)
 
 
 def gram_kernel(embed_ref, gram_ref):
@@ -256,6 +254,21 @@
         copy.wait()
 
 
+def gather(block, axis, size):
+    return lax.all_to_all(jnp.broadcast_to(block, (size,) + block.shape), axis, 0, 0)
+
+
+def along_y_x(block):
+    column = gather(block, "y", N_Y).reshape(N_Y * 8, HALF)
+    return gather(column, "x", N_X).reshape(BATCH, HALF)
+
+
+def along_x_y(block):
+    line = gather(block, "x", N_X).reshape(N_X * 8, HALF)
+    batch = gather(line, "y", N_Y).reshape(N_Y, N_X, 8, HALF)
+    return batch.transpose(1, 0, 2, 3).reshape(BATCH, HALF)
+
+
 def local(hidden, segment_ids, assign, positive, gain):
     shape = jax.ShapeDtypeStruct
     gain = gain.reshape(1, D)
@@ -281,6 +294,7 @@
             compiler_params=PARAMS,
         )(*[pltpu.with_memory_space_constraint(v, pltpu.HBM) for v in (hidden, segment_ids, assign, gain, positive.T)])
     with jax.named_scope("pooled_to_relay"):
+        send, core = lax.optimization_barrier((send, lax.axis_index("core")))
         pooled = lax.all_to_all(send.reshape(2 * N_ZL, 8, -1), ("core", "zl"), 0, 0)
         pooled = pooled.reshape(2 * N_ZL * 8, -1)
     with jax.named_scope("relay"):
@@ -296,15 +310,14 @@
     with jax.named_scope("owned"):
         send, embed = pl.pallas_call(
             owned_kernel,
-            out_shape=(shape((N_Y, 8, HALF), BF16), shape((8, HALF), F32)),
+            out_shape=(shape((8, HALF), BF16), shape((8, HALF), F32)),
             in_specs=[VMEM],
             out_specs=(VMEM, VMEM),
             compiler_params=PARAMS,
         )(pooled)
     with jax.named_scope("embed_exchange"):
-        batch = lax.all_to_all(send, "y", 0, 0).reshape(N_Y * 8, HALF)
-        batch = jnp.broadcast_to(batch, (N_X, N_Y * 8, HALF))
-        batch = lax.all_to_all(batch, "x", 0, 0).reshape(BATCH, HALF)
+        send, core = lax.optimization_barrier((send, core))
+        batch = lax.cond(core == 0, along_y_x, along_x_y, send)
     with jax.named_scope("gram"):
         gram = pl.pallas_call(
             gram_kernel,

time: 103 us -> 100 us (0.971)
  blocking collectives: 94.9 us -> 92.3 us
    all_gather x1, blocking collectives: 5.92 us -> 2.31 us  [local(): gram = lax.all_gather(gram, 'core', axis=0)]
    all_to_all x1, blocking collectives: 10.4 us -> 11.9 us  [local(): grads = lax.all_to_all(send, 'zh', 0, 0).reshape(N_ZH * 8, HALF)]
where the time goes in v6:
time: 100 us
  blocking collectives  92.3 us (92%)
  Pallas kernels  6.75 us (7%)
    all_to_all x2, blocking collectives, gather(): lax.all_to_all(jnp.broadcast_to(block, (size,) + block.shape), axis, 0, 0)  33 us
    all_to_all x1, blocking collectives, local(): pooled = lax.all_to_all(send.reshape(2 * N_ZL, 8, -1), ('core', 'zl'), 0, 0)  19.7 us
    all_to_all x1, blocking collectives, local(): pooled = lax.all_to_all(send, 'zh', 0, 0)  15.4 us
    all_to_all x1, blocking collectives, local(): grads = lax.all_to_all(send, 'zh', 0, 0).reshape(N_ZH * 8, HALF)  11.9 us
    all_to_all x1, blocking collectives, local(): lax.all_to_all(send.reshape(2 * N_ZL, 8, QUARTER), ('core', 'zl'), 0, 0)  9.9 us
    pallas_call x1, Pallas kernels, local(): pl.pallas_call(pool_kernel, out_shape=(shape((2, N_ZL, 8, QUARTER + META)...  2.61 us
    pallas_call x1, Pallas kernels, local(): pl.pallas_call(rows_kernel, out_shape=shape((1, ROWS, D), BF16), in_specs...  2.4 us
    all_gather x1, blocking collectives, local(): gram = lax.all_gather(gram, 'core', axis=0)  2.31 us

profile of v6, /device:TPU:1, one launch (start us, length us, event | category | flops | bytes accessed | tf_op | source)
XLA Modules:
  0.0 100.0 jit_solution(7700270665927813272)
XLA Ops:
  0.6 2.6 %pool.1 = (bf16[2,4,8,1152]{3,2,1,0:T(8,128)(2,1)S(1)}, f32[256,128]{1,0:T(8,128)S(1)}, s32[1,256]{1,0:T(1,128)S(1)}) custom-call(bf16[1,256,4096]{2,1,0:T(8,128)(2,1)} %hidden_ref.1, s32[1,1,256]{2,1,0:T(1,128)} %segment_ref.1, s32[1,4]{1,0:T(1,128)} %assign_hbm.1, f32[1,4096]{1,0:T(1,128)} %bitcast.21, s32[4,64]{1,0:T(4,128)} %bitcast.28), custom_call_target="tpu_custom_call" | custom-call | tf_op jit(solution)/shard_map/pool/pallas_call | solution.py:276
  3.2 19.7 %all_to_all.40 = bf16[8,8,1152]{2,1,0:T(8,128)(2,1)S(1)} all-to-all(bf16[8,8,1152]{2,1,0:T(8,128)(2,1)S(1)} %bitcast.20), channel_id=1, replica_groups=mesh['x'=4,'y'=8,'core'=2,'zh'=3,'zl'=4] {'core','zl'}, dimensions={0} | all-to-all | bytes 294912 | tf_op jit(solution)/shard_map/pooled_to_relay/all_to_all | solution.py:298
  23.0 0.2 relay.1
  23.1 15.4 %all_to_all.41.pooled_ref = bf16[3,8,2048]{2,1,0:T(8,128)(2,1)S(1)} all-to-all(bf16[3,8,2048]{2,1,0:T(8,128)(2,1)S(1)} %get-tuple-element.22), channel_id=1, replica_groups=mesh['x'=4,'y'=8,'core'=2,'zh'=3,'zl'=4] {'zh'}, dimensions={0} | all-to-all | bytes 196608 | tf_op jit(solution)/shard_map/pooled_to_owner/all_to_all | solution.py:309
  38.6 33.3 %conditional.1 = (bf16[256,2048]{1,0:T(8,128)(2,1)S(1)}) conditional(s32[]{:T(128)} %convert_element_type.3, bf16[8,2048]{1,0:T(8,128)(2,1)S(1)} %get-tuple-element.26, bf16[8,2048]{1,0:T(8,128)(2,1)S(1)} %get-tuple-element.26), branch_computations={%region_0.0_spmd, %region_1.0_spmd} | conditional | bytes 5799944 | solution.py:320
  38.6 8.6 %all_to_all.36 = bf16[4,8,2048]{2,1,0:T(8,128)(2,1)S(1)} all-to-all(bf16[4,8,2048]{2,1,0:T(8,128)(2,1)S(1)} %broadcast_in_dim.8), channel_id=1, replica_groups=mesh['x'=4,'y'=8,'core'=2,'zh'=3,'zl'=4] {'x'}, dimensions={0} | all-to-all | bytes 262144 | tf_op jit(solution)/shard_map/embed_exchange/cond/branch_0_fun/all_to_all | solution.py:258
  47.3 0.1 broadcast_in_dim.9
  47.4 24.4 %all_to_all.37 = bf16[8,32,2048]{2,1,0:T(8,128)(2,1)S(1)} all-to-all(bf16[8,32,2048]{2,1,0:T(8,128)(2,1)S(1)} %broadcast_in_dim.9), channel_id=1, replica_groups=mesh['x'=4,'y'=8,'core'=2,'zh'=3,'zl'=4] {'y'}, dimensions={0} | all-to-all | bytes 2097152 | tf_op jit(solution)/shard_map/embed_exchange/cond/branch_0_fun/all_to_all | solution.py:258
  71.8 0.1 copy.7
  71.9 0.0 copy-start
  71.9 0.0 copy-start.1
  71.9 0.0 copy-start.2
  71.9 0.5 gram.1
  72.4 2.3 %all-gather = f32[512,256]{1,0:T(8,128)S(1)} all-gather(f32[256,256]{1,0:T(8,128)S(1)} %gram.1), channel_id=2, replica_groups=mesh['x'=4,'y'=8,'core'=2,'zh'=3,'zl'=4] {'core'}, dimensions={0}, use_global_device_ids=true | all-gather | bytes 786432 | tf_op jit(solution)/shard_map/gram/all_gather | solution.py:329
  74.7 0.9 contrast.1
  75.6 11.9 %all_to_all.42 = bf16[3,8,2048]{2,1,0:T(8,128)(2,1)S(1)} all-to-all(bf16[3,8,2048]{2,1,0:T(8,128)(2,1)S(1)} %get-tuple-element.30), channel_id=1, replica_groups=mesh['x'=4,'y'=8,'core'=2,'zh'=3,'zl'=4] {'zh'}, dimensions={0} | all-to-all | bytes 196608 | tf_op jit(solution)/shard_map/grad_to_relay/all_to_all | solution.py:339
  87.5 0.2 back.1
  87.7 9.9 %all_to_all.43 = bf16[8,8,1024]{2,1,0:T(8,128)(2,1)S(1)} all-to-all(bf16[8,8,1024]{2,1,0:T(8,128)(2,1)S(1)} %bitcast.18), channel_id=1, replica_groups=mesh['x'=4,'y'=8,'core'=2,'zh'=3,'zl'=4] {'core','zl'}, dimensions={0} | all-to-all | bytes 262144 | tf_op jit(solution)/shard_map/grad_to_rows/all_to_all | solution.py:349
  97.6 0.0 copy-done
  97.6 0.0 copy-done.1
  97.6 0.0 copy-done.2
  97.6 2.4 %rows.1 = bf16[1,256,4096]{2,1,0:T(8,128)(2,1)} custom-call(bf16[2,4,8,1024]{3,2,1,0:T(8,128)(2,1)S(1)} %bitcast.17, bf16[1,256,4096]{2,1,0:T(8,128)(2,1)S(1)} %copy-done, s32[1,1,256]{2,1,0:T(1,128)S(1)} %copy-done.2, f32[1,4096]{1,0:T(1,128)S(1)} %bitcast.22, f32[256,128]{1,0:T(8,128)S(1)} %get-tuple-element.32.upright_ref), custom_call_target="tpu_custom_call" | custom-call | tf_op jit(solution)/shard_map/rows/pallas_call | solution.py:352
  (2 shorter events, 0.0 us)
Async XLA Ops:
  71.9 25.8 %copy-start = (bf16[1,256,4096]{2,1,0:T(8,128)(2,1)S(1)}, bf16[1,256,4096]{2,1,0:T(8,128)(2,1)}, u32[]{:S(2)}) copy-start(bf16[1,256,4096]{2,1,0:T(8,128)(2,1)} %hidden_ref.1) | copy-start | bytes 6291460
  71.9 25.7 %copy-start.1 = (f32[4096]{0:T(1024)S(1)}, f32[4096]{0:T(1024)}, u32[]{:S(2)}) copy-start(f32[4096]{0:T(1024)} %param.11) | copy-start | bytes 49156
  71.9 25.7 %copy-start.2 = (s32[1,1,256]{2,1,0:T(1,128)S(1)}, s32[1,1,256]{2,1,0:T(1,128)}, u32[]{:S(2)}) copy-start(s32[1,1,256]{2,1,0:T(1,128)} %segment_ref.1) | copy-start | bytes 3076

commit v7 on v6

--- a/solution.py
+++ b/solution.py
@@ -19,7 +19,7 @@
 HALF = D // 2
 QUARTER = D // 4
 PAS = 4
-CHUNK = 1024
+CHUNK = 2048
 BLOCK = 64
 META = 128
 N_ZH = 3
@@ -80,11 +80,11 @@
     owner = jnp.zeros((8, META), jnp.int32)
     for k in range(PAS):
         owner = jnp.where(lax.rem(row, PAS) == k, assign_at[0:1, k : k + 1], owner)
-    place = lax.axis_index("core") * 32 + lax.axis_index("zl") * 8 + row
+    place = lax.axis_index("zl") * 16 + lax.axis_index("core") * 8 + row
     meta = jnp.where(iota((8, META), 1) == place, owner, 0).astype(F32).astype(BF16)
     for h in range(2):
         for peer in range(N_ZL):
-            send_ref[h, peer, :, QUARTER:] = meta
+            send_ref[peer, h, :, QUARTER:] = meta
     lane = iota((64, BATCH), 1)
     spread = jnp.where(lax.div(lane, PAS) == iota((64, BATCH), 0), 1.0, 0.0).astype(BF16)
     partner = jnp.concatenate([positive[...].astype(F32), jnp.zeros((PAS, 64), F32)], axis=0)
@@ -107,7 +107,7 @@
         pooled = (pooled * gain[:, columns] / counts)[0:PAS]
         pooled = jnp.concatenate([pooled[:, 0:QUARTER], pooled[:, QUARTER:]], axis=0).astype(BF16)
         for peer in range(N_ZL):
-            send_ref[h, peer, :, 0:QUARTER] = pooled
+            send_ref[peer, h, :, 0:QUARTER] = pooled
     upright_ref[...] = jnp.concatenate(
         [onehot, onehot, onehot, inverse, jnp.zeros((96, ROWS), F32)], axis=0
     ).T
@@ -119,7 +119,7 @@
     row = iota((128, META), 0)
     lane = iota((128, META), 1)
     slot = (lax.div(row, 8) * N_ZL + relay) * PAS + lax.rem(row, PAS)
-    hit = (owners == slot.astype(F32)) & (lax.div(lane, 32) == lax.div(lax.rem(row, 8), PAS))
+    hit = (owners == slot.astype(F32)) & (lax.rem(lax.div(lane, 8), 2) == lax.div(lax.rem(row, 8), PAS))
     hit = hit & (row < N_ZH * 8) & (lane < 64)
     select = jnp.where(hit, 1.0, 0.0)
     back_ref[...] = select.T
@@ -206,10 +206,10 @@
             preferred_element_type=F32,
         )
     total = total.astype(BF16)
-    for c in range(2):
-        for peer in range(N_ZL):
-            at = (c * N_ZL + peer) * 8
-            send_ref[c, peer] = total[at : at + 8]
+    for peer in range(N_ZL):
+        for c in range(2):
+            at = (peer * 2 + c) * 8
+            send_ref[peer, c] = total[at : at + 8]
 
 
 def rows_kernel(
@@ -220,9 +220,9 @@
     onehot = jnp.where(segment == iota((8, ROWS), 0), 1.0, 0.0)
     counts = jnp.maximum(jnp.sum(onehot, axis=1, keepdims=True), 1.0)
     for h in range(2):
-        part = grad_ref[h, 0].astype(F32)
+        part = grad_ref[0, h].astype(F32)
         for peer in range(1, N_ZL):
-            part = part + grad_ref[h, peer].astype(F32)
+            part = part + grad_ref[peer, h].astype(F32)
         for q in range(2):
             columns = pl.ds((h * 2 + q) * QUARTER, QUARTER)
             scaled[:, columns] = split3(gain_ref[:, columns] * (part / counts))
@@ -276,7 +276,7 @@
         send, upright, partner = pl.pallas_call(
             pool_kernel,
             out_shape=(
-                shape((2, N_ZL, 8, QUARTER + META), BF16),
+                shape((N_ZL, 2, 8, QUARTER + META), BF16),
                 shape((ROWS, 128), F32),
                 shape((1, BATCH), jnp.int32),
             ),
@@ -295,8 +295,8 @@
         )(*[pltpu.with_memory_space_constraint(v, pltpu.HBM) for v in (hidden, segment_ids, assign, gain, positive.T)])
     with jax.named_scope("pooled_to_relay"):
         send, core = lax.optimization_barrier((send, lax.axis_index("core")))
-        pooled = lax.all_to_all(send.reshape(2 * N_ZL, 8, -1), ("core", "zl"), 0, 0)
-        pooled = pooled.reshape(2 * N_ZL * 8, -1)
+        pooled = lax.all_to_all(send.reshape(N_ZL * 2, 8, -1), ("zl", "core"), 0, 0)
+        pooled = pooled.reshape(N_ZL * 2 * 8, -1)
     with jax.named_scope("relay"):
         send, back = pl.pallas_call(
             relay_kernel,
@@ -340,14 +340,14 @@
     with jax.named_scope("back"):
         send = pl.pallas_call(
             back_kernel,
-            out_shape=shape((2, N_ZL, 8, QUARTER), BF16),
+            out_shape=shape((N_ZL, 2, 8, QUARTER), BF16),
             in_specs=[VMEM, VMEM],
             out_specs=VMEM,
             compiler_params=PARAMS,
         )(grads, back)
     with jax.named_scope("grad_to_rows"):
-        grads = lax.all_to_all(send.reshape(2 * N_ZL, 8, QUARTER), ("core", "zl"), 0, 0)
-        grads = grads.reshape(2, N_ZL, 8, QUARTER)
+        grads = lax.all_to_all(send.reshape(N_ZL * 2, 8, QUARTER), ("zl", "core"), 0, 0)
+        grads = grads.reshape(N_ZL, 2, 8, QUARTER)
     with jax.named_scope("rows"):
         grad_rows = pl.pallas_call(
             rows_kernel,

time: 100 us -> 99.7 us (level)
    all_gather x1, blocking collectives: 2.31 us -> 4.33 us  [local(): gram = lax.all_gather(gram, 'core', axis=0)]
    all_to_all x1, blocking collectives: 15.4 us -> 13.5 us  [local(): pooled = lax.all_to_all(send, 'zh', 0, 0)]
    all_to_all x1, blocking collectives: 11.9 us -> 10 us  [local(): grads = lax.all_to_all(send, 'zh', 0, 0).reshape(N_ZH * 8, HALF)]
    all_to_all x2, blocking collectives: 29.6 us -> 31 us  [the longest x1 18.8 us: local(): pooled = lax.all_to_all(send.reshape(N_ZL * 2, 8, -1), ('zl', 'core'), 0, 0)]
where the time goes in v7:
time: 99.7 us; the launch traced here: 99.3 us
  blocking collectives  91.8 us (92%)
  Pallas kernels  6.55 us (7%)
    all_to_all x2, blocking collectives, gather(): lax.all_to_all(jnp.broadcast_to(block, (size,) + block.shape), axis, 0, 0)  33 us
    all_to_all x1, blocking collectives, local(): pooled = lax.all_to_all(send.reshape(N_ZL * 2, 8, -1), ('zl', 'core'), 0, 0)  18.8 us
    all_to_all x1, blocking collectives, local(): pooled = lax.all_to_all(send, 'zh', 0, 0)  13.5 us
    all_to_all x1, blocking collectives, local(): lax.all_to_all(send.reshape(N_ZL * 2, 8, QUARTER), ('zl', 'core'), 0, 0)  12.2 us
    all_to_all x1, blocking collectives, local(): grads = lax.all_to_all(send, 'zh', 0, 0).reshape(N_ZH * 8, HALF)  10 us
    all_gather x1, blocking collectives, local(): gram = lax.all_gather(gram, 'core', axis=0)  4.33 us
    pallas_call x1, Pallas kernels, local(): pl.pallas_call(pool_kernel, out_shape=(shape((N_ZL, 2, 8, QUARTER + META)...  2.41 us
    pallas_call x1, Pallas kernels, local(): pl.pallas_call(rows_kernel, out_shape=shape((1, ROWS, D), BF16), in_specs...  2.4 us

profile of v7, /device:TPU:1, one launch (start us, length us, event | category | flops | bytes accessed | tf_op | source)
XLA Modules:
  0.0 99.3 jit_solution(5348626302374020281)
XLA Ops:
  0.6 2.4 %pool.1 = (bf16[4,2,8,1152]{3,2,1,0:T(8,128)(2,1)S(1)}, f32[256,128]{1,0:T(8,128)S(1)}, s32[1,256]{1,0:T(1,128)S(1)}) custom-call(bf16[1,256,4096]{2,1,0:T(8,128)(2,1)} %hidden_ref.1, s32[1,1,256]{2,1,0:T(1,128)} %segment_ref.1, s32[1,4]{1,0:T(1,128)} %assign_hbm.1, f32[1,4096]{1,0:T(1,128)} %bitcast.21, s32[4,64]{1,0:T(4,128)} %bitcast.28), custom_call_target="tpu_custom_call" | custom-call | tf_op jit(solution)/shard_map/pool/pallas_call | solution.py:276
  3.0 18.8 %all_to_all.40 = bf16[8,8,1152]{2,1,0:T(8,128)(2,1)S(1)} all-to-all(bf16[8,8,1152]{2,1,0:T(8,128)(2,1)S(1)} %bitcast.20), channel_id=1, replica_groups=mesh['x'=4,'y'=8,'core'=2,'zh'=3,'zl'=4] {'zl','core'}, dimensions={0} | all-to-all | bytes 294912 | tf_op jit(solution)/shard_map/pooled_to_relay/all_to_all | solution.py:298
  21.9 0.2 relay.1
  22.0 13.5 %all_to_all.41.pooled_ref = bf16[3,8,2048]{2,1,0:T(8,128)(2,1)S(1)} all-to-all(bf16[3,8,2048]{2,1,0:T(8,128)(2,1)S(1)} %get-tuple-element.22), channel_id=1, replica_groups=mesh['x'=4,'y'=8,'core'=2,'zh'=3,'zl'=4] {'zh'}, dimensions={0} | all-to-all | bytes 196608 | tf_op jit(solution)/shard_map/pooled_to_owner/all_to_all | solution.py:309
  35.5 33.3 %conditional.1 = (bf16[256,2048]{1,0:T(8,128)(2,1)S(1)}) conditional(s32[]{:T(128)} %convert_element_type.3, bf16[8,2048]{1,0:T(8,128)(2,1)S(1)} %get-tuple-element.26, bf16[8,2048]{1,0:T(8,128)(2,1)S(1)} %get-tuple-element.26), branch_computations={%region_0.0_spmd, %region_1.0_spmd} | conditional | bytes 5799944 | solution.py:320
  35.5 8.6 %all_to_all.36 = bf16[4,8,2048]{2,1,0:T(8,128)(2,1)S(1)} all-to-all(bf16[4,8,2048]{2,1,0:T(8,128)(2,1)S(1)} %broadcast_in_dim.8), channel_id=1, replica_groups=mesh['x'=4,'y'=8,'core'=2,'zh'=3,'zl'=4] {'x'}, dimensions={0} | all-to-all | bytes 262144 | tf_op jit(solution)/shard_map/embed_exchange/cond/branch_0_fun/all_to_all | solution.py:258
  44.2 0.1 broadcast_in_dim.9
  44.3 24.4 %all_to_all.37 = bf16[8,32,2048]{2,1,0:T(8,128)(2,1)S(1)} all-to-all(bf16[8,32,2048]{2,1,0:T(8,128)(2,1)S(1)} %broadcast_in_dim.9), channel_id=1, replica_groups=mesh['x'=4,'y'=8,'core'=2,'zh'=3,'zl'=4] {'y'}, dimensions={0} | all-to-all | bytes 2097152 | tf_op jit(solution)/shard_map/embed_exchange/cond/branch_0_fun/all_to_all | solution.py:258
  68.7 0.1 copy.7
  68.8 0.0 copy-start
  68.8 0.0 copy-start.1
  68.8 0.0 copy-start.2
  68.8 0.5 gram.1
  69.3 4.3 %all-gather = f32[512,256]{1,0:T(8,128)S(1)} all-gather(f32[256,256]{1,0:T(8,128)S(1)} %gram.1), channel_id=2, replica_groups=mesh['x'=4,'y'=8,'core'=2,'zh'=3,'zl'=4] {'core'}, dimensions={0}, use_global_device_ids=true | all-gather | bytes 786432 | tf_op jit(solution)/shard_map/gram/all_gather | solution.py:329
  73.6 0.9 contrast.1
  74.5 10.0 %all_to_all.42 = bf16[3,8,2048]{2,1,0:T(8,128)(2,1)S(1)} all-to-all(bf16[3,8,2048]{2,1,0:T(8,128)(2,1)S(1)} %get-tuple-element.30), channel_id=1, replica_groups=mesh['x'=4,'y'=8,'core'=2,'zh'=3,'zl'=4] {'zh'}, dimensions={0} | all-to-all | bytes 196608 | tf_op jit(solution)/shard_map/grad_to_relay/all_to_all | solution.py:339
  84.6 0.2 back.1
  84.8 12.2 %all_to_all.43 = bf16[8,8,1024]{2,1,0:T(8,128)(2,1)S(1)} all-to-all(bf16[8,8,1024]{2,1,0:T(8,128)(2,1)S(1)} %bitcast.18), channel_id=1, replica_groups=mesh['x'=4,'y'=8,'core'=2,'zh'=3,'zl'=4] {'zl','core'}, dimensions={0} | all-to-all | bytes 262144 | tf_op jit(solution)/shard_map/grad_to_rows/all_to_all | solution.py:349
  96.9 0.0 copy-done
  96.9 0.0 copy-done.1
  96.9 0.0 copy-done.2
  96.9 2.4 %rows.1 = bf16[1,256,4096]{2,1,0:T(8,128)(2,1)} custom-call(bf16[4,2,8,1024]{3,2,1,0:T(8,128)(2,1)S(1)} %bitcast.17, bf16[1,256,4096]{2,1,0:T(8,128)(2,1)S(1)} %copy-done, s32[1,1,256]{2,1,0:T(1,128)S(1)} %copy-done.2, f32[1,4096]{1,0:T(1,128)S(1)} %bitcast.22, f32[256,128]{1,0:T(8,128)S(1)} %get-tuple-element.32.upright_ref), custom_call_target="tpu_custom_call" | custom-call | tf_op jit(solution)/shard_map/rows/pallas_call | solution.py:352
  (2 shorter events, 0.0 us)
Async XLA Ops:
  68.8 28.1 %copy-start = (bf16[1,256,4096]{2,1,0:T(8,128)(2,1)S(1)}, bf16[1,256,4096]{2,1,0:T(8,128)(2,1)}, u32[]{:S(2)}) copy-start(bf16[1,256,4096]{2,1,0:T(8,128)(2,1)} %hidden_ref.1) | copy-start | bytes 6291460
  68.8 28.1 %copy-start.1 = (f32[4096]{0:T(1024)S(1)}, f32[4096]{0:T(1024)}, u32[]{:S(2)}) copy-start(f32[4096]{0:T(1024)} %param.11) | copy-start | bytes 49156
  68.8 28.1 %copy-start.2 = (s32[1,1,256]{2,1,0:T(1,128)S(1)}, s32[1,1,256]{2,1,0:T(1,128)}, u32[]{:S(2)}) copy-start(s32[1,1,256]{2,1,0:T(1,128)} %segment_ref.1) | copy-start | bytes 3076

commit v8 on v7

--- a/solution.py
+++ b/solution.py
@@ -150,7 +150,8 @@
 
 def contrast_kernel(gram_ref, batch_ref, embed_ref, partner_ref, loss_ref, send_ref):
     core = lax.axis_index("core")
-    first = (lax.axis_index("x") * 8 + lax.axis_index("y")) * 8
+    first = lax.axis_index("xh") * 2 + lax.axis_index("xl")
+    first = ((first * 4 + lax.axis_index("yh")) * 2 + lax.axis_index("yl")) * 8
     shift = inv_tau
     row = iota((8, BATCH), 0)
     lane = iota((8, BATCH), 1)
@@ -258,15 +259,19 @@
     return lax.all_to_all(jnp.broadcast_to(block, (size,) + block.shape), axis, 0, 0)
 
 
+Y_AXES, X_AXES = ("yl", "yh"), ("xh", "xl")
+
+
 def along_y_x(block):
-    column = gather(block, "y", N_Y).reshape(N_Y * 8, HALF)
-    return gather(column, "x", N_X).reshape(BATCH, HALF)
+    column = gather(block, Y_AXES, N_Y).reshape(2, 4, 8, HALF).swapaxes(0, 1).reshape(N_Y * 8, HALF)
+    return gather(column, X_AXES, N_X).reshape(BATCH, HALF)
 
 
 def along_x_y(block):
-    line = gather(block, "x", N_X).reshape(N_X * 8, HALF)
-    batch = gather(line, "y", N_Y).reshape(N_Y, N_X, 8, HALF)
-    return batch.transpose(1, 0, 2, 3).reshape(BATCH, HALF)
+    line = gather(block, X_AXES, N_X).reshape(N_X * 8, HALF)
+    batch = gather(line, Y_AXES, N_Y)
+    batch = batch.reshape((2, 4) + (N_X, 8, HALF)).transpose(2, 1, 0, 3, 4)
+    return batch.reshape(BATCH, HALF)
 
 
 def local(hidden, segment_ids, assign, positive, gain):
@@ -367,9 +372,10 @@
 
 def solution(mesh):
     fine = Mesh(
-        mesh.devices.reshape(N_X, N_Y, 2, N_ZH, N_ZL), ("x", "y", "core", "zh", "zl")
+        mesh.devices.reshape(2, 2, 4, 2, 2, N_ZH, N_ZL),
+        ("xh", "xl", "yh", "yl", "core", "zh", "zl"),
     )
-    group, dp = ("x", "y", "core"), ("zh", "zl")
+    group, dp = ("xh", "xl", "yh", "yl", "core"), ("zh", "zl")
     placed = (P(group, dp, None), P(group, dp, None), P(group, dp), P(None, dp), P())
     return jax.shard_map(
         local,

time: 99.7 us -> 97.7 us (0.980)
  blocking collectives: 91.8 us -> 89.8 us
    all_to_all x2, blocking collectives: 33 us -> 31.4 us  [gather(): lax.all_to_all(jnp.broadcast_to(block, (size,) + block.shape), axis, 0, 0)]
where the time goes in v8:
time: 97.7 us; the launch traced here: 97.3 us
  blocking collectives  89.8 us (92%)
  Pallas kernels  6.55 us (7%)
    all_to_all x2, blocking collectives, gather(): lax.all_to_all(jnp.broadcast_to(block, (size,) + block.shape), axis, 0, 0)  31.4 us
    all_to_all x1, blocking collectives, local(): pooled = lax.all_to_all(send.reshape(N_ZL * 2, 8, -1), ('zl', 'core'), 0, 0)  18.8 us
    all_to_all x1, blocking collectives, local(): pooled = lax.all_to_all(send, 'zh', 0, 0)  13.5 us
    all_to_all x1, blocking collectives, local(): lax.all_to_all(send.reshape(N_ZL * 2, 8, QUARTER), ('zl', 'core'), 0, 0)  12.1 us
    all_to_all x1, blocking collectives, local(): grads = lax.all_to_all(send, 'zh', 0, 0).reshape(N_ZH * 8, HALF)  10 us
    all_gather x1, blocking collectives, local(): gram = lax.all_gather(gram, 'core', axis=0)  3.96 us
    pallas_call x1, Pallas kernels, local(): pl.pallas_call(pool_kernel, out_shape=(shape((N_ZL, 2, 8, QUARTER + META)...  2.41 us
    pallas_call x1, Pallas kernels, local(): pl.pallas_call(rows_kernel, out_shape=shape((1, ROWS, D), BF16), in_specs...  2.4 us

profile of v8, /device:TPU:1, one launch (start us, length us, event | category | flops | bytes accessed | tf_op | source)
XLA Modules:
  0.0 97.3 jit_solution(12633957474956159198)
XLA Ops:
  0.6 2.4 %pool.1 = (bf16[4,2,8,1152]{3,2,1,0:T(8,128)(2,1)S(1)}, f32[256,128]{1,0:T(8,128)S(1)}, s32[1,256]{1,0:T(1,128)S(1)}) custom-call(bf16[1,256,4096]{2,1,0:T(8,128)(2,1)} %hidden_ref.1, s32[1,1,256]{2,1,0:T(1,128)} %segment_ref.1, s32[1,4]{1,0:T(1,128)} %assign_hbm.1, f32[1,4096]{1,0:T(1,128)} %bitcast.24, s32[4,64]{1,0:T(4,128)} %bitcast.32), custom_call_target="tpu_custom_call" | custom-call | tf_op jit(solution)/shard_map/pool/pallas_call | solution.py:281
  3.0 18.8 %all_to_all.40 = bf16[8,8,1152]{2,1,0:T(8,128)(2,1)S(1)} all-to-all(bf16[8,8,1152]{2,1,0:T(8,128)(2,1)S(1)} %bitcast.23), channel_id=1, replica_groups=mesh['xh'=2,'xl'=2,'yh'=4,'yl'=2,'core'=2,'zh'=3,'zl'=4] {'zl','core'}, dimensions={0} | all-to-all | bytes 294912 | tf_op jit(solution)/shard_map/pooled_to_relay/all_to_all | solution.py:303
  21.9 0.2 relay.1
  22.0 13.5 %all_to_all.41.pooled_ref = bf16[3,8,2048]{2,1,0:T(8,128)(2,1)S(1)} all-to-all(bf16[3,8,2048]{2,1,0:T(8,128)(2,1)S(1)} %get-tuple-element.22), channel_id=1, replica_groups=mesh['xh'=2,'xl'=2,'yh'=4,'yl'=2,'core'=2,'zh'=3,'zl'=4] {'zh'}, dimensions={0} | all-to-all | bytes 196608 | tf_op jit(solution)/shard_map/pooled_to_owner/all_to_all | solution.py:314
  35.5 31.7 %conditional.1 = (bf16[256,2048]{1,0:T(8,128)(2,1)S(1)}) conditional(s32[]{:T(128)} %convert_element_type.3, bf16[8,2048]{1,0:T(8,128)(2,1)S(1)} %get-tuple-element.26, bf16[8,2048]{1,0:T(8,128)(2,1)S(1)} %get-tuple-element.26), branch_computations={%region_0.0_spmd, %region_1.0_spmd} | conditional | bytes 5799944 | solution.py:325
  35.5 8.6 %all_to_all.36 = bf16[4,8,2048]{2,1,0:T(8,128)(2,1)S(1)} all-to-all(bf16[4,8,2048]{2,1,0:T(8,128)(2,1)S(1)} %broadcast_in_dim.8), channel_id=1, replica_groups=mesh['xh'=2,'xl'=2,'yh'=4,'yl'=2,'core'=2,'zh'=3,'zl'=4] {'xh','xl'}, dimensions={0} | all-to-all | bytes 262144 | tf_op jit(solution)/shard_map/embed_exchange/cond/branch_0_fun/all_to_all | solution.py:259
  44.2 0.1 broadcast_in_dim.9
  44.3 22.8 %all_to_all.37 = bf16[8,32,2048]{2,1,0:T(8,128)(2,1)S(1)} all-to-all(bf16[8,32,2048]{2,1,0:T(8,128)(2,1)S(1)} %broadcast_in_dim.9), channel_id=1, replica_groups=mesh['xh'=2,'xl'=2,'yh'=4,'yl'=2,'core'=2,'zh'=3,'zl'=4] {'yl','yh'}, dimensions={0} | all-to-all | bytes 2097152 | tf_op jit(solution)/shard_map/embed_exchange/cond/branch_0_fun/all_to_all | solution.py:259
  67.1 0.1 copy.7
  67.2 0.0 copy-start
  67.2 0.0 copy-start.1
  67.2 0.0 copy-start.2
  67.2 0.5 gram.1
  67.7 4.0 %all-gather = f32[512,256]{1,0:T(8,128)S(1)} all-gather(f32[256,256]{1,0:T(8,128)S(1)} %gram.1), channel_id=2, replica_groups=mesh['xh'=2,'xl'=2,'yh'=4,'yl'=2,'core'=2,'zh'=3,'zl'=4] {'core'}, dimensions={0}, use_global_device_ids=true | all-gather | bytes 786432 | tf_op jit(solution)/shard_map/gram/all_gather | solution.py:334
  71.7 0.9 contrast.1
  72.5 10.0 %all_to_all.42 = bf16[3,8,2048]{2,1,0:T(8,128)(2,1)S(1)} all-to-all(bf16[3,8,2048]{2,1,0:T(8,128)(2,1)S(1)} %get-tuple-element.30), channel_id=1, replica_groups=mesh['xh'=2,'xl'=2,'yh'=4,'yl'=2,'core'=2,'zh'=3,'zl'=4] {'zh'}, dimensions={0} | all-to-all | bytes 196608 | tf_op jit(solution)/shard_map/grad_to_relay/all_to_all | solution.py:344
  82.6 0.2 back.1
  82.8 12.1 %all_to_all.43 = bf16[8,8,1024]{2,1,0:T(8,128)(2,1)S(1)} all-to-all(bf16[8,8,1024]{2,1,0:T(8,128)(2,1)S(1)} %bitcast.21), channel_id=1, replica_groups=mesh['xh'=2,'xl'=2,'yh'=4,'yl'=2,'core'=2,'zh'=3,'zl'=4] {'zl','core'}, dimensions={0} | all-to-all | bytes 262144 | tf_op jit(solution)/shard_map/grad_to_rows/all_to_all | solution.py:354
  94.9 0.0 copy-done
  94.9 0.0 copy-done.1
  94.9 0.0 copy-done.2
  94.9 2.4 %rows.1 = bf16[1,256,4096]{2,1,0:T(8,128)(2,1)} custom-call(bf16[4,2,8,1024]{3,2,1,0:T(8,128)(2,1)S(1)} %bitcast.20, bf16[1,256,4096]{2,1,0:T(8,128)(2,1)S(1)} %copy-done, s32[1,1,256]{2,1,0:T(1,128)S(1)} %copy-done.2, f32[1,4096]{1,0:T(1,128)S(1)} %bitcast.25, f32[256,128]{1,0:T(8,128)S(1)} %get-tuple-element.32.upright_ref), custom_call_target="tpu_custom_call" | custom-call | tf_op jit(solution)/shard_map/rows/pallas_call | solution.py:357
  (2 shorter events, 0.0 us)
Async XLA Ops:
  67.2 27.7 %copy-start = (bf16[1,256,4096]{2,1,0:T(8,128)(2,1)S(1)}, bf16[1,256,4096]{2,1,0:T(8,128)(2,1)}, u32[]{:S(2)}) copy-start(bf16[1,256,4096]{2,1,0:T(8,128)(2,1)} %hidden_ref.1) | copy-start | bytes 6291460
  67.2 27.7 %copy-start.1 = (f32[4096]{0:T(1024)S(1)}, f32[4096]{0:T(1024)}, u32[]{:S(2)}) copy-start(f32[4096]{0:T(1024)} %param.11) | copy-start | bytes 49156
  67.2 27.7 %copy-start.2 = (s32[1,1,256]{2,1,0:T(1,128)S(1)}, s32[1,1,256]{2,1,0:T(1,128)}, u32[]{:S(2)}) copy-start(s32[1,1,256]{2,1,0:T(1,128)} %segment_ref.1) | copy-start | bytes 3076

commit v9 on v8

--- a/solution.py
+++ b/solution.py
@@ -80,7 +80,8 @@
     owner = jnp.zeros((8, META), jnp.int32)
     for k in range(PAS):
         owner = jnp.where(lax.rem(row, PAS) == k, assign_at[0:1, k : k + 1], owner)
-    place = lax.axis_index("zl") * 16 + lax.axis_index("core") * 8 + row
+    place = (lax.axis_index("zb") * 2 + lax.axis_index("za")) * 16
+    place = place + lax.axis_index("core") * 8 + row
     meta = jnp.where(iota((8, META), 1) == place, owner, 0).astype(F32).astype(BF16)
     for h in range(2):
         for peer in range(N_ZL):
@@ -114,7 +115,7 @@
 
 
 def relay_kernel(pooled_ref, send_ref, back_ref):
-    relay = lax.axis_index("zl")
+    relay = lax.axis_index("za") * 2 + lax.axis_index("zb")
     owners = jnp.sum(pooled_ref[:, QUARTER:].astype(F32), axis=0, keepdims=True)
     row = iota((128, META), 0)
     lane = iota((128, META), 1)
@@ -300,7 +301,7 @@
         )(*[pltpu.with_memory_space_constraint(v, pltpu.HBM) for v in (hidden, segment_ids, assign, gain, positive.T)])
     with jax.named_scope("pooled_to_relay"):
         send, core = lax.optimization_barrier((send, lax.axis_index("core")))
-        pooled = lax.all_to_all(send.reshape(N_ZL * 2, 8, -1), ("zl", "core"), 0, 0)
+        pooled = lax.all_to_all(send.reshape(N_ZL * 2, 8, -1), ("zb", "za", "core"), 0, 0)
         pooled = pooled.reshape(N_ZL * 2 * 8, -1)
     with jax.named_scope("relay"):
         send, back = pl.pallas_call(
@@ -351,7 +352,7 @@
             compiler_params=PARAMS,
         )(grads, back)
     with jax.named_scope("grad_to_rows"):
-        grads = lax.all_to_all(send.reshape(N_ZL * 2, 8, QUARTER), ("zl", "core"), 0, 0)
+        grads = lax.all_to_all(send.reshape(N_ZL * 2, 8, QUARTER), ("zb", "za", "core"), 0, 0)
         grads = grads.reshape(N_ZL, 2, 8, QUARTER)
     with jax.named_scope("rows"):
         grad_rows = pl.pallas_call(
@@ -372,10 +373,10 @@
 
 def solution(mesh):
     fine = Mesh(
-        mesh.devices.reshape(2, 2, 4, 2, 2, N_ZH, N_ZL),
-        ("xh", "xl", "yh", "yl", "core", "zh", "zl"),
+        mesh.devices.reshape(2, 2, 4, 2, 2, N_ZH, 2, 2),
+        ("xh", "xl", "yh", "yl", "core", "zh", "za", "zb"),
     )
-    group, dp = ("xh", "xl", "yh", "yl", "core"), ("zh", "zl")
+    group, dp = ("xh", "xl", "yh", "yl", "core"), ("zh", "za", "zb")
     placed = (P(group, dp, None), P(group, dp, None), P(group, dp), P(None, dp), P())
     return jax.shard_map(
         local,

time: 97.7 us -> 97.7 us (level)
    all_to_all x2, blocking collectives: 30.9 us -> 27.7 us  [the longest x1 18.8 us: local(): lax.all_to_all(send.reshape(N_ZL * 2, 8, -1), ('zb', 'za', 'core'), 0, 0)]
    all_to_all x1, blocking collectives: 10 us -> 13.3 us  [local(): grads = lax.all_to_all(send, 'zh', 0, 0).reshape(N_ZH * 8, HALF)]
where the time goes in v9:
time: 97.7 us; the launch traced here: 97.2 us
  blocking collectives  89.7 us (92%)
  Pallas kernels  6.54 us (7%)
    all_to_all x2, blocking collectives, gather(): lax.all_to_all(jnp.broadcast_to(block, (size,) + block.shape), axis, 0, 0)  31.4 us
    all_to_all x1, blocking collectives, local(): lax.all_to_all(send.reshape(N_ZL * 2, 8, -1), ('zb', 'za', 'core'), 0, 0)  18.8 us
    all_to_all x1, blocking collectives, local(): pooled = lax.all_to_all(send, 'zh', 0, 0)  13.3 us
    all_to_all x1, blocking collectives, local(): grads = lax.all_to_all(send, 'zh', 0, 0).reshape(N_ZH * 8, HALF)  13.3 us
    all_to_all x1, blocking collectives, local(): lax.all_to_all(send.reshape(N_ZL * 2, 8, QUARTER), ('zb', 'za', 'core'),...  8.81 us
    all_gather x1, blocking collectives, local(): gram = lax.all_gather(gram, 'core', axis=0)  4.04 us
    pallas_call x1, Pallas kernels, local(): pl.pallas_call(pool_kernel, out_shape=(shape((N_ZL, 2, 8, QUARTER + META)...  2.41 us
    pallas_call x1, Pallas kernels, local(): pl.pallas_call(rows_kernel, out_shape=shape((1, ROWS, D), BF16), in_specs...  2.4 us

profile of v9, /device:TPU:1, one launch (start us, length us, event | category | flops | bytes accessed | tf_op | source)
XLA Modules:
  0.0 97.2 jit_solution(8673348506507662383)
XLA Ops:
  0.6 2.4 %pool.1 = (bf16[4,2,8,1152]{3,2,1,0:T(8,128)(2,1)S(1)}, f32[256,128]{1,0:T(8,128)S(1)}, s32[1,256]{1,0:T(1,128)S(1)}) custom-call(bf16[1,256,4096]{2,1,0:T(8,128)(2,1)} %hidden_ref.1, s32[1,1,256]{2,1,0:T(1,128)} %segment_ref.1, s32[1,4]{1,0:T(1,128)} %assign_hbm.1, f32[1,4096]{1,0:T(1,128)} %bitcast.24, s32[4,64]{1,0:T(4,128)} %bitcast.32), custom_call_target="tpu_custom_call" | custom-call | tf_op jit(solution)/shard_map/pool/pallas_call | solution.py:282
  3.0 18.8 %all_to_all.40 = bf16[8,8,1152]{2,1,0:T(8,128)(2,1)S(1)} all-to-all(bf16[8,8,1152]{2,1,0:T(8,128)(2,1)S(1)} %bitcast.23), channel_id=1, replica_groups=mesh['xh'=2,'xl'=2,'yh'=4,'yl'=2,'core'=2,'zh'=3,'za'=2,'zb'=2] {'zb','z..., dimensions={0} | all-to-all | bytes 294912 | tf_op jit(solution)/shard_map/pooled_to_relay/all_to_all | solution.py:304
  21.9 0.2 relay.1
  22.1 13.3 %all_to_all.41.pooled_ref = bf16[3,8,2048]{2,1,0:T(8,128)(2,1)S(1)} all-to-all(bf16[3,8,2048]{2,1,0:T(8,128)(2,1)S(1)} %get-tuple-element.22), channel_id=1, replica_groups=mesh['xh'=2,'xl'=2,'yh'=4,'yl'=2,'core'=2,'zh'=3,'za'=2,'zb'=2] {'zh'}, dimensions={0} | all-to-all | bytes 196608 | tf_op jit(solution)/shard_map/pooled_to_owner/all_to_all | solution.py:315
  35.4 31.7 %conditional.1 = (bf16[256,2048]{1,0:T(8,128)(2,1)S(1)}) conditional(s32[]{:T(128)} %convert_element_type.3, bf16[8,2048]{1,0:T(8,128)(2,1)S(1)} %get-tuple-element.26, bf16[8,2048]{1,0:T(8,128)(2,1)S(1)} %get-tuple-element.26), branch_computations={%region_0.0_spmd, %region_1.0_spmd} | conditional | bytes 5799944 | solution.py:326
  35.4 8.6 %all_to_all.36 = bf16[4,8,2048]{2,1,0:T(8,128)(2,1)S(1)} all-to-all(bf16[4,8,2048]{2,1,0:T(8,128)(2,1)S(1)} %broadcast_in_dim.8), channel_id=1, replica_groups=mesh['xh'=2,'xl'=2,'yh'=4,'yl'=2,'core'=2,'zh'=3,'za'=2,'zb'=2] {'xh','xl'}, dimensions={0} | all-to-all | bytes 262144 | tf_op jit(solution)/shard_map/embed_exchange/cond/branch_0_fun/all_to_all | solution.py:260
  44.1 0.1 broadcast_in_dim.9
  44.2 22.8 %all_to_all.37 = bf16[8,32,2048]{2,1,0:T(8,128)(2,1)S(1)} all-to-all(bf16[8,32,2048]{2,1,0:T(8,128)(2,1)S(1)} %broadcast_in_dim.9), channel_id=1, replica_groups=mesh['xh'=2,'xl'=2,'yh'=4,'yl'=2,'core'=2,'zh'=3,'za'=2,'zb'=2] {'yl','yh'}, dimensions={0} | all-to-all | bytes 2097152 | tf_op jit(solution)/shard_map/embed_exchange/cond/branch_0_fun/all_to_all | solution.py:260
  66.9 0.1 copy.7
  67.1 0.0 copy-start
  67.1 0.0 copy-start.1
  67.1 0.0 copy-start.2
  67.1 0.5 gram.1
  67.6 4.0 %all-gather = f32[512,256]{1,0:T(8,128)S(1)} all-gather(f32[256,256]{1,0:T(8,128)S(1)} %gram.1), channel_id=2, replica_groups=mesh['xh'=2,'xl'=2,'yh'=4,'yl'=2,'core'=2,'zh'=3,'za'=2,'zb'=2] {'core'}, dimensions={0}, use_global_device_ids=true | all-gather | bytes 786432 | tf_op jit(solution)/shard_map/gram/all_gather | solution.py:335
  71.6 0.9 contrast.1
  72.5 13.3 %all_to_all.42 = bf16[3,8,2048]{2,1,0:T(8,128)(2,1)S(1)} all-to-all(bf16[3,8,2048]{2,1,0:T(8,128)(2,1)S(1)} %get-tuple-element.30), channel_id=1, replica_groups=mesh['xh'=2,'xl'=2,'yh'=4,'yl'=2,'core'=2,'zh'=3,'za'=2,'zb'=2] {'zh'}, dimensions={0} | all-to-all | bytes 196608 | tf_op jit(solution)/shard_map/grad_to_relay/all_to_all | solution.py:345
  85.8 0.2 back.1
  86.0 8.8 %all_to_all.43 = bf16[8,8,1024]{2,1,0:T(8,128)(2,1)S(1)} all-to-all(bf16[8,8,1024]{2,1,0:T(8,128)(2,1)S(1)} %bitcast.21), channel_id=1, replica_groups=mesh['xh'=2,'xl'=2,'yh'=4,'yl'=2,'core'=2,'zh'=3,'za'=2,'zb'=2] {'zb','z..., dimensions={0} | all-to-all | bytes 262144 | tf_op jit(solution)/shard_map/grad_to_rows/all_to_all | solution.py:355
  94.8 0.0 copy-done
  94.8 0.0 copy-done.1
  94.8 0.0 copy-done.2
  94.8 2.4 %rows.1 = bf16[1,256,4096]{2,1,0:T(8,128)(2,1)} custom-call(bf16[4,2,8,1024]{3,2,1,0:T(8,128)(2,1)S(1)} %bitcast.20, bf16[1,256,4096]{2,1,0:T(8,128)(2,1)S(1)} %copy-done, s32[1,1,256]{2,1,0:T(1,128)S(1)} %copy-done.2, f32[1,4096]{1,0:T(1,128)S(1)} %bitcast.25, f32[256,128]{1,0:T(8,128)S(1)} %get-tuple-element.32.upright_ref), custom_call_target="tpu_custom_call" | custom-call | tf_op jit(solution)/shard_map/rows/pallas_call | solution.py:358
  (2 shorter events, 0.0 us)
Async XLA Ops:
  67.1 27.7 %copy-start = (bf16[1,256,4096]{2,1,0:T(8,128)(2,1)S(1)}, bf16[1,256,4096]{2,1,0:T(8,128)(2,1)}, u32[]{:S(2)}) copy-start(bf16[1,256,4096]{2,1,0:T(8,128)(2,1)} %hidden_ref.1) | copy-start | bytes 6291460
  67.1 27.7 %copy-start.1 = (f32[4096]{0:T(1024)S(1)}, f32[4096]{0:T(1024)}, u32[]{:S(2)}) copy-start(f32[4096]{0:T(1024)} %param.11) | copy-start | bytes 49156
  67.1 27.7 %copy-start.2 = (s32[1,1,256]{2,1,0:T(1,128)S(1)}, s32[1,1,256]{2,1,0:T(1,128)}, u32[]{:S(2)}) copy-start(s32[1,1,256]{2,1,0:T(1,128)} %segment_ref.1) | copy-start | bytes 3076
